TPU v7x, 256 devices: a whole 4x4x8 slice. The times are simulated.
256 devices in a mesh: expert: 64 (over y, z, core), replica: 4 (over x).
Axes of the slice: x: 4, y: 4, z: 8, core: 2. Of those that a mesh axis runs over, the one named last changes fastest.
Arguments:
- tokens: bfloat16 [8192, 4096], P('expert', 'replica'), may hold values from -6 to 6
- probs: float32 [8192, 8], P('expert'), may hold values from 0.02 to 0.3
- expert_ids: int32 [8192, 8], P('expert'), may hold values from 0 to 63, all different within a row; in each aligned block of 128 rows (0 to 127, 128 to 255, ...) at most 20 rows name the same one
- grad_out: bfloat16 [8192, 4096], P('expert', 'replica'), may hold values from -6 to 6
- w_gate: bfloat16 [64, 4096, 768], P('expert', 'replica'), may hold values from -0.09375 to 0.09375
- w_up: bfloat16 [64, 4096, 768], P('expert', 'replica'), may hold values from -0.09375 to 0.09375
- w_down: bfloat16 [64, 768, 4096], P('expert', None, 'replica'), may hold values from -0.21875 to 0.21875
Outputs:
- mixed: bfloat16 [8192, 4096], P('expert', 'replica')
- grad_tokens: bfloat16 [8192, 4096], P('expert', 'replica')
- grad_gate: bfloat16 [64, 4096, 768], P('expert', 'replica')
- grad_up: bfloat16 [64, 4096, 768], P('expert', 'replica')
- grad_down: bfloat16 [64, 768, 4096], P('expert', None, 'replica')
Inputs may be any that keep to these rules, and one draw needn't show every extreme that they name: `expert_ids`: the 8 ids of a token differ. Among the entries of the 128 tokens of one index of the expert axis, no expert is named more than 20 times, a bound that some block reaches.
All inputs are finite; a program needn't handle non-finite values.
Results may differ from a plain program's by a relative error of at most 0.024.
Values may be sent and summed in bfloat16 or wider, within the bound.
No kernel may reach another device: no remote copies, remote signals or barrier semaphores. Data moves between devices by JAX's collectives and lax.ppermute only.
A program may use at most 128 MiB of HBM per device.

v0:
```python
import jax
import jax.numpy as jnp
from jax import lax
from jax.experimental import pallas as pl
from jax.experimental.pallas import tpu as pltpu
from jax.sharding import Mesh, PartitionSpec as P

BF = jnp.bfloat16
F32 = jnp.float32
NY, NZ, NC, NX = 4, 8, 2, 4
DEST = NY * NC
CAP = 20
SLOTS = NZ * CAP
ROWS = DEST * SLOTS
QUARTER = ROWS // NX
TILE = 256
VMEM, MOST = 40 * 2**20, 60 * 2**20
OFFSETS = (0, -1, 1, -2, 2, -3, 3, 4)
NB = NZ // 2
PART = ROWS // 2


def shift(value, axis, by):
    n = {"y": NY, "z": NZ, "core": NC, "x": NX}[axis]
    return lax.ppermute(value, axis, [(i, (i + by) % n) for i in range(n)])


def after(value, *others):
    return lax.optimization_barrier((value,) + others)[0]


def dot(a, b, contract=((1,), (0,))):
    return lax.dot_general(a, b, (contract, ((), ())), preferred_element_type=F32)


def struct(shape, dtype=BF):
    return jax.ShapeDtypeStruct(shape, dtype)


def whole(a):
    return pl.BlockSpec(a.shape, lambda *_: (0,) * len(a.shape))


def columns(a):
    return pl.BlockSpec((a.shape[0], TILE), lambda i, *_: (0, i))


def rows_of(a, n):
    return pl.BlockSpec((a.shape[0] // n, a.shape[1]), lambda i, *_: (i, 0))


def turned_rows(a):
    return pl.BlockSpec((a.shape[0] // NX, a.shape[1]), lambda i, x: (lax.rem(x[0] + i, NX), 0))


def call(body, grid, args, in_specs, outs, out_specs, scratch=(), x=None, vmem=VMEM):
    spec = pltpu.PrefetchScalarGridSpec(
        num_scalar_prefetch=0 if x is None else 1,
        grid=(grid,),
        in_specs=in_specs,
        out_specs=out_specs,
        scratch_shapes=list(scratch),
    )
    return pl.pallas_call(
        body,
        out_shape=outs,
        grid_spec=spec,
        compiler_params=pltpu.CompilerParams(vmem_limit_bytes=vmem),
        cost_estimate=pl.CostEstimate(flops=1, bytes_accessed=1, transcendentals=0),
    )(*([] if x is None else [x]), *args)


def pick_body(scaled, place_ref, *refs):
    data_ref, out_ref, hot_ref, scale_ref = refs[-4:]
    for d in range(DEST):
        part = pl.ds(d * SLOTS, SLOTS)
        hot = place_ref[d][None, :] == lax.broadcasted_iota(jnp.int32, (SLOTS, hot_ref.shape[1]), 0)
        hot_ref[part, :] = jnp.where(hot, 1.0, 0.0).astype(BF)
        if scaled:
            weight = jnp.where(hot, refs[0][d][None, :], 0.0)
            scale_ref[part, :] = jnp.sum(weight, axis=1, keepdims=True)
    rows = dot(hot_ref[...], data_ref[...])
    out_ref[...] = (rows * scale_ref[...] if scaled else rows).astype(BF)


def pick(place, data, weight=None):
    args = [place, data] if weight is None else [place, weight, data]
    out = struct((ROWS, data.shape[1]))
    return call(
        lambda *refs: pick_body(weight is not None, *refs),
        1,
        args,
        [whole(a) for a in args],
        out,
        whole(out),
        [pltpu.VMEM((ROWS, data.shape[0]), BF), pltpu.VMEM((ROWS, 1), F32)],
    )


def mix_body(weighted, place_ref, *refs):
    rows_ref, out_ref = refs[-2:]
    rows = rows_ref.shape[0]
    slots = rows // DEST
    owner = lax.broadcasted_iota(jnp.int32, (DEST, rows), 1) // slots
    spread = jnp.where(owner == lax.broadcasted_iota(jnp.int32, (DEST, rows), 0), 1.0, 0.0).astype(BF)
    shape = (out_ref.shape[0], rows)
    spot = (lax.broadcasted_iota(jnp.int32, shape, 1) % slots).astype(F32)
    hot = dot(place_ref[...], spread) == spot
    value = jnp.where(hot, dot(refs[0][...], spread) if weighted else 1.0, 0.0)
    out_ref[...] = dot(value.astype(BF), rows_ref[...]).astype(BF)


def mix(place, rows, weight=None):
    tables = [t.T.astype(BF) for t in ([place] if weight is None else [place, weight])]
    tokens = tables[0].shape[0]
    out = struct((tokens, rows.shape[1]))
    return call(
        lambda *refs: mix_body(weight is not None, *refs),
        2,
        tables + [rows],
        [rows_of(t, 2) for t in tables] + [whole(rows)],
        out,
        rows_of(out, 2),
    )


def gate_up_body(rows_ref, gate_ref, up_ref, out_ref):
    tiles = pl.num_programs(0) // 2

    @pl.when(pl.program_id(0) < tiles)
    def _():
        out_ref[...] = dot(rows_ref[...], gate_ref[...]).astype(BF)

    @pl.when(pl.program_id(0) >= tiles)
    def _():
        out_ref[...] = dot(rows_ref[...], up_ref[...]).astype(BF)


def hidden_body(sums_ref, hidden_ref):
    hid = hidden_ref.shape[1]
    gate = sums_ref[:, :hid].astype(F32)
    hidden_ref[...] = (gate / (1.0 + jnp.exp(-gate)) * sums_ref[:, hid:].astype(F32)).astype(BF)


def back_body(x_ref, rows_ref, down_ref, *outs):
    part = dot(rows_ref[...], down_ref[...], ((1,), (1,))).astype(BF)
    for i, out in enumerate(outs):

        @pl.when(pl.program_id(0) == i)
        def _():
            out[...] = part


def grads_body(a, b, c, d, sums_ref, *outs):
    hid = a.shape[1]
    back = a[...].astype(F32) + b[...].astype(F32) + c[...].astype(F32) + d[...].astype(F32)
    gate, up = sums_ref[:, :hid].astype(F32), sums_ref[:, hid:].astype(F32)
    sigma = 1.0 / (1.0 + jnp.exp(-gate))
    grad_a = (back * up * sigma * (1.0 + gate * (1.0 - sigma))).astype(BF)
    grad_b = (back * gate * sigma).astype(BF)
    size = SLOTS // 2
    for n in range(QUARTER // size):
        out, part = outs[n % 2], pl.ds(n // 2 * size, size)
        out[part, :hid] = grad_a[n * size : (n + 1) * size]
        out[part, hid:] = grad_b[n * size : (n + 1) * size]


def out_body(hidden_ref, down_ref, out_ref):
    out_ref[...] = dot(hidden_ref[...], down_ref[...]).astype(BF)


def input_body(x_ref, *refs):
    pieces, (gate_w, up_w, rows_ref, both_ref) = refs[:NX], refs[NX:]
    hid = gate_w.shape[1]
    size = pieces[0].shape[0]
    for i, piece in enumerate(pieces):
        start = lax.rem(x_ref[0] + i, NX) * size
        both_ref[pl.ds(pl.multiple_of(start, size), size), :] = piece[...]
    rows = dot(both_ref[:, :hid], gate_w[...], ((1,), (1,))) + dot(both_ref[:, hid:], up_w[...], ((1,), (1,)))
    rows_ref[...] = rows.astype(BF)


def outer_body(left_ref, right_ref, out_ref):
    out_ref[...] = dot(left_ref[...], right_ref[...], ((0,), (0,))).astype(BF)


def outer(left, right):
    out = struct((left.shape[1], right.shape[1]))
    return call(
        outer_body, right.shape[1] // TILE, [left, right], [whole(left), columns(right)], out, columns(out)
    )


def outer_chunks_body(near_ref, far_ref, near_both, far_both, out_ref):
    width = near_ref.shape[2]
    near = dot(near_ref[...].reshape(PART, width), near_both[...], ((0,), (0,)))
    out_ref[...] = (near + dot(far_ref[...].reshape(PART, width), far_both[...], ((0,), (0,)))).astype(BF)


def outer_chunks(rows, near, far, tiles, skip):
    rows = rows.reshape(DEST, SLOTS, -1)
    out = struct((rows.shape[2], tiles * TILE))
    half = (DEST, SLOTS // 2, rows.shape[2])
    return call(
        outer_chunks_body,
        tiles,
        [rows, rows, near, far],
        [
            pl.BlockSpec(half, lambda i: (0, 0, 0)),
            pl.BlockSpec(half, lambda i: (0, 1, 0)),
            pl.BlockSpec((PART, TILE), lambda i: (0, i + skip)),
            pl.BlockSpec((PART, TILE), lambda i: (0, i + skip)),
        ],
        out,
        columns(out),
    )


def routing(probs, expert_ids):
    z = lax.axis_index("z")
    top = expert_ids.shape[1]
    meta = jnp.concatenate([expert_ids.astype(F32).T, probs.T], 0)
    meta = jnp.broadcast_to(meta[None], (NZ,) + meta.shape)
    meta = lax.all_to_all(meta, "z", 0, 0, tiled=True)
    ids, weight = meta[:, :top], meta[:, top:]
    dest = jnp.arange(DEST)
    mine = ((dest // NC * NZ + z) * NC + dest % NC).astype(F32)
    match = ids[None] == mine[:, None, None, None]
    member = jnp.any(match, axis=2)
    weight = jnp.sum(jnp.where(match, weight[None], 0.0), axis=2)
    tok = ids.shape[-1]
    earlier = (jnp.arange(tok)[:, None] < jnp.arange(tok)[None, :]).astype(BF)
    slot = dot(member.astype(BF).reshape(-1, tok), earlier).reshape(member.shape)
    return jnp.where(member, slot, -1000.0), weight


def plus(a, b):
    return (a.astype(F32) + b.astype(F32)).astype(BF)


def per_device(tokens, probs, expert_ids, grad_out, w_gate, w_up, w_down):
    gate_w, up_w, down_w = w_gate[0], w_up[0], w_down[0]
    width, hid = gate_w.shape
    tok = tokens.shape[0]
    x = lax.axis_index("x").astype(jnp.int32).reshape(1)
    z = lax.axis_index("z")

    def swap(rows):
        got = lax.all_to_all(rows.reshape(DEST, -1, width), ("y", "core"), 0, 0, tiled=True)
        return got.reshape(rows.shape)

    all_tokens = lax.all_gather(tokens, "z", axis=0, tiled=True)
    slot, weight = routing(probs, expert_ids)
    turn = jnp.array([OFFSETS.index((d + 3) % NZ - 3) for d in range(NZ)])
    turn = jnp.take(turn, (jnp.arange(NZ) - z) % NZ)
    place = (slot + (turn * CAP).astype(F32)[None, :, None]).reshape(DEST, NZ * tok)
    weight = weight.reshape(DEST, NZ * tok)
    listed = jnp.take(slot, (z + jnp.array(OFFSETS)) % NZ, axis=1)
    listed = listed + (jnp.arange(NZ) % NB * CAP).astype(F32)[None, :, None]
    near_place, far_place = (listed[:, c * NB : (c + 1) * NB].reshape(DEST, NB * tok) for c in range(2))
    table = place.astype(jnp.int32)
    all_grads = lax.all_gather(after(grad_out, all_tokens, table), "z", axis=0, tiled=True)

    rows = swap(pick(table, all_tokens))
    sums = struct((ROWS, 2 * hid))
    tiles = hid // TILE
    sums = call(
        gate_up_body,
        2 * tiles,
        [rows, gate_w, up_w],
        [
            whole(rows),
            pl.BlockSpec((width, TILE), lambda i: (0, jnp.minimum(i, tiles - 1))),
            pl.BlockSpec((width, TILE), lambda i: (0, jnp.maximum(i - tiles, 0))),
        ],
        sums,
        columns(sums),
    )
    picked = pick(after(table, sums), all_grads, weight)
    sums = lax.psum_scatter(sums, "x", scatter_dimension=0, tiled=True)
    grads = swap(picked)
    quarter = struct((QUARTER, hid))
    pieces = call(
        back_body,
        NX,
        [grads, down_w],
        [turned_rows(grads), whole(down_w)],
        [quarter] * NX,
        [whole(quarter)] * NX,
        x=x,
    )
    sums = after(sums, pieces[0])
    hidden = call(hidden_body, 1, [sums], [whole(sums)], quarter, whole(quarter))
    hidden = lax.all_gather(hidden, "x", axis=0, tiled=True)
    pieces = [pieces[0], shift(pieces[1], "x", 1), shift(pieces[2], "x", 2), shift(pieces[3], "x", -1)]
    out = struct((ROWS, width))
    out_rows = call(
        out_body,
        NX,
        [after(hidden, *pieces), down_w],
        [rows_of(hidden, NX), whole(down_w)],
        out,
        rows_of(out, NX),
        vmem=MOST,
    )
    mixed_rows = swap(out_rows)
    pieces[0] = after(pieces[0], out_rows)
    both = struct((QUARTER // 2, 2 * hid))
    near, far = call(
        grads_body, 1, pieces + [sums], [whole(p) for p in pieces] + [whole(sums)], [both] * 2, [whole(both)] * 2, vmem=MOST
    )
    near, far = ([own, shift(own, "x", -1), shift(own, "x", 2), shift(own, "x", 1)] for own in (near, far))

    def to_input(pieces, turn):
        out, both = struct((PART, width)), struct((PART, 2 * hid))
        return call(
            input_body,
            1,
            pieces + [gate_w, up_w],
            [whole(p) for p in pieces] + [whole(gate_w), whole(up_w)],
            [out, both],
            [whole(out), whole(both)],
            x=after(x, turn),
            vmem=MOST,
        )

    far_input, far = to_input(far, near[3])
    far_rows = swap(after(far_input, mixed_rows))
    mixed = mix(after(place, far_input), mixed_rows, weight)
    far_sums = mix(after(far_place, mixed), far_rows)
    near_input, near = to_input(near, far_sums)
    near_rows = swap(after(near_input, far_rows))
    mixed = lax.psum_scatter(mixed, "z", scatter_dimension=0, tiled=True)
    grad_gate = outer_chunks(rows, near, far, tiles, 0)
    grad_up = outer_chunks(rows, near, after(far, grad_gate), tiles, tiles)
    near_sums = mix(near_place, after(near_rows, grad_up))
    grad_down = outer(after(hidden, near_sums), grads)

    at = {o: far_sums[i * tok : (i + 1) * tok] for i, o in enumerate(OFFSETS[NB:])}
    at.update((o, near_sums[i * tok : (i + 1) * tok]) for i, o in enumerate(OFFSETS[:NB]))
    half = tok // 2
    low, high = shift(at[4][:half], "z", 1), shift(at[4][half:], "z", -1)
    up = shift(jnp.concatenate([plus(at[3][:half], low), at[3][half:]], 0), "z", 1)
    down = shift(jnp.concatenate([at[-3][:half], plus(at[-3][half:], high)], 0), "z", -1)
    for step in (2, 1):
        up, down = shift(plus(at[step], up), "z", 1), shift(plus(at[-step], down), "z", -1)
    grad_tokens = (at[0].astype(F32) + up.astype(F32) + down.astype(F32)).astype(BF)
    return (mixed, grad_tokens, grad_gate[None], grad_up[None], grad_down[None])


def solution(mesh):
    split = Mesh(mesh.devices.reshape(NY, NZ, NC, NX), ("y", "z", "core", "x"))
    e, x = ("y", "z", "core"), "x"
    in_specs = (P(e, x), P(e, None), P(e, None), P(e, x), P(e, x, None), P(e, x, None), P(e, None, x))
    out_specs = (P(e, x), P(e, x), P(e, x, None), P(e, x, None), P(e, None, x))
    return jax.shard_map(per_device, mesh=split, in_specs=in_specs, out_specs=out_specs, check_vma=False)
```

profile of v0, /device:TPU:1, one launch (start us, length us, event | category | flops | bytes accessed | tf_op | source)
XLA Modules:
  0.0 359.2 jit_solution(14661121753310531476)
XLA Ops:
  9.9 9.0 %all-to-all-start = ((f32[8,16,128]{2,1,0:T(8,128)}), f32[8,16,128]{2,1,0:T(8,128)S(1)}, u32[]{:S(2)}, u32[]{:S(2)}) async-start(f32[8,16,128]{2,1,0:T(8,128)} %broadcast_in_dim.52), calls=%async_computation | async-start | bytes 131072 | tf_op jit(solution)/shard_map/all_to_all | solution.py:224
  19.0 1.3 gather_fusion
  20.3 5.8 %all-to-all-done = f32[8,16,128]{2,1,0:T(8,128)S(1)} async-done(((f32[8,16,128]{2,1,0:T(8,128)}), f32[8,16,128]{2,1,0:T(8,128)S(1)}, u32[]{:S(2)}, u32[]{:S(2)}) %all-to-all-start) | async-done | bytes 65568 | tf_op jit(solution)/shard_map/all_to_all | solution.py:224
  26.8 24.3 %all-gather.4.cloned.1.call-done.refs_1_ = bf16[1024,1024]{1,0:T(8,128)(2,1)} async-done(((bf16[128,1024]{1,0:T(8,128)(2,1)}), bf16[1024,1024]{1,0:T(8,128)(2,1)}) %all-gather.4.cloned.1.call-update) | async-done | bytes 2097168 | tf_op jit(solution)/shard_map/all_gather | solution.py:252
  51.3 1.6 copy-done.11
  52.9 2.9 shard_map.128
  55.8 40.9 %all_to_all.30.near_ref.far_ref = bf16[8,160,1024]{2,1,0:T(8,128)(2,1)S(1)} all-to-all(bf16[8,160,1024]{2,1,0:T(8,128)(2,1)S(1)} %bitcast.53), channel_id=1, replica_groups=mesh['y'=4,'z'=8,'core'=2,'x'=4] {'y','core'}, dimensions={0} | all-to-all | bytes 5242880 | tf_op jit(solution)/shard_map/all_to_all | solution.py:249
  96.7 5.8 %shard_map.129 = bf16[1280,1536]{1,0:T(8,128)(2,1)S(1)} custom-call(bf16[1280,1024]{1,0:T(8,128)(2,1)S(1)} %bitcast.45, bf16[1024,768]{1,0:T(8,128)(2,1)S(1)} %bitcast.48, bf16[1024,768]{1,0:T(8,128)(2,1)S(1)} %bitcast.51), custom_call_target="tpu_custom_call" | custom-call | flops 1 | bytes 1 | tf_op jit(solution)/shard_map/pallas_call | solution.py:64
  102.5 2.0 copy-done
  104.9 0.8 copy-done.18
  105.8 1.2 copy.30.refs_0_
  107.1 1.6 copy-done.12
  108.6 3.3 shard_map.130
  111.9 1.6 copy-done.3
  113.5 5.3 %all-to-all-start.2 = ((bf16[8,160,1024]{2,1,0:T(8,128)(2,1)}), bf16[8,160,1024]{2,1,0:T(8,128)(2,1)}, u32[]{:S(2)}, u32[]{:S(2)}) async-start(bf16[8,160,1024]{2,1,0:T(8,128)(2,1)} %bitcast.52), calls=%async_computation.2 | async-start | bytes 5242880 | tf_op jit(solution)/shard_map/all_to_all | solution.py:249
  118.8 32.1 %all-to-all-done.2 = bf16[8,160,1024]{2,1,0:T(8,128)(2,1)} async-done(((bf16[8,160,1024]{2,1,0:T(8,128)(2,1)}), bf16[8,160,1024]{2,1,0:T(8,128)(2,1)}, u32[]{:S(2)}, u32[]{:S(2)}) %all-to-all-start.2) | async-done | bytes 2621472 | tf_op jit(solution)/shard_map/all_to_all | solution.py:249
  150.9 1.4 copy-done.8
  152.3 4.6 %shard_map.131 = (bf16[320,768]{1,0:T(8,128)(2,1)S(1)}, bf16[320,768]{1,0:T(8,128)(2,1)S(1)}, bf16[320,768]{1,0:T(8,128)(2,1)S(1)}, bf16[320,768]{1,0:T(8,128)(2,1)S(1)}) custom-call(s32[1]{0:T(128)} %bitcast.5.x_ref, bf16[1280,1024]{1,0:T(8,128)(2,1)} %bitcast.12.rows_ref.right_ref, bf16[768,1024]{1,0:T(8,128)(2,1)S(1)} %bitcast.55), custom_call_target="tpu_custom_call" | custom-call | flops 1 | bytes 1 | tf_op jit(solution)/shard_map/pallas_call | solution.py:64
  157.7 0.8 copy-done.14
  158.5 0.8 copy-done.15
  159.2 1.2 copy-done.10
  160.4 1.1 shard_map.132
  161.6 1.3 collective-permute-start
  162.8 2.4 collective-permute-start.1
  165.2 1.2 collective-permute-start.2
  166.4 8.6 %collective-permute-done.b = bf16[320,768]{1,0:T(8,128)(2,1)} collective-permute-done((bf16[320,768]{1,0:T(8,128)(2,1)}, bf16[320,768]{1,0:T(8,128)(2,1)}, u32[]{:S(2)}, u32[]{:S(2)}) %collective-permute-start) | collective-permute-done | bytes 491552 | tf_op jit(solution)/shard_map/ppermute | solution.py:25
  175.0 22.2 %collective-permute-done.1.c = bf16[320,768]{1,0:T(8,128)(2,1)} collective-permute-done((bf16[320,768]{1,0:T(8,128)(2,1)}, bf16[320,768]{1,0:T(8,128)(2,1)}, u32[]{:S(2)}, u32[]{:S(2)}) %collective-permute-start.1) | collective-permute-done | bytes 491552 | tf_op jit(solution)/shard_map/ppermute | solution.py:25
  197.2 6.4 %all-gather.8.cloned.1.call-done.hidden_ref.left_ref = bf16[1280,768]{1,0:T(8,128)(2,1)} async-done(((bf16[320,768]{1,0:T(8,128)(2,1)}), bf16[1280,768]{1,0:T(8,128)(2,1)}) %all-gather.8.cloned.1.call-update) | async-done | bytes 1966096 | tf_op jit(solution)/shard_map/all_gather | solution.py:294
  203.6 5.8 %shard_map.133 = bf16[1280,1024]{1,0:T(8,128)(2,1)} custom-call(bf16[1280,768]{1,0:T(8,128)(2,1)} %all-gather.8.cloned.1.call-done.hidden_ref.left_ref, bf16[768,1024]{1,0:T(8,128)(2,1)} %bitcast.54), custom_call_target="tpu_custom_call" | custom-call | flops 1 | bytes 1 | tf_op jit(solution)/shard_map/pallas_call | solution.py:64
  209.3 4.9 %all-to-all-start.3 = ((bf16[8,160,1024]{2,1,0:T(8,128)(2,1)}), bf16[8,160,1024]{2,1,0:T(8,128)(2,1)}, u32[]{:S(2)}, u32[]{:S(2)}) async-start(bf16[8,160,1024]{2,1,0:T(8,128)(2,1)} %bitcast.58), calls=%async_computation.4 | async-start | bytes 5242880 | tf_op jit(solution)/shard_map/all_to_all | solution.py:249
  214.2 3.4 shard_map.134
  217.6 1.2 collective-permute-start.3
  218.8 1.5 collective-permute-start.4
  220.3 1.5 collective-permute-start.5
  222.0 9.7 %collective-permute-done.3.refs_3_ = bf16[160,1536]{1,0:T(8,128)(2,1)} collective-permute-done((bf16[160,1536]{1,0:T(8,128)(2,1)}, bf16[160,1536]{1,0:T(8,128)(2,1)}, u32[]{:S(2)}, u32[]{:S(2)}) %collective-permute-start.3) | collective-permute-done | bytes 491552 | tf_op jit(solution)/shard_map/ppermute | solution.py:25
  231.8 11.4 %collective-permute-done.5.refs_2_ = bf16[160,1536]{1,0:T(8,128)(2,1)} collective-permute-done((bf16[160,1536]{1,0:T(8,128)(2,1)}, bf16[160,1536]{1,0:T(8,128)(2,1)}, u32[]{:S(2)}, u32[]{:S(2)}) %collective-permute-start.5) | collective-permute-done | bytes 491552 | tf_op jit(solution)/shard_map/ppermute | solution.py:25
  243.2 9.6 %collective-permute-done.6.refs_3_ = bf16[160,1536]{1,0:T(8,128)(2,1)} collective-permute-done((bf16[160,1536]{1,0:T(8,128)(2,1)}, bf16[160,1536]{1,0:T(8,128)(2,1)}, u32[]{:S(2)}, u32[]{:S(2)}) %collective-permute-start.6) | collective-permute-done | bytes 491552 | tf_op jit(solution)/shard_map/ppermute | solution.py:25
  252.9 5.8 %shard_map.135 = (bf16[640,1024]{1,0:T(8,128)(2,1)}, bf16[640,1536]{1,0:T(8,128)(2,1)}) custom-call(s32[1]{0:T(128)} %bitcast.5.x_ref, bf16[160,1536]{1,0:T(8,128)(2,1)} %get-tuple-element.40.refs_0_, bf16[160,1536]{1,0:T(8,128)(2,1)} %collective-permute-done.4.refs_1_, bf16[160,1536]{1,0:T(8,128)(2,1)} %collective-permute-done.5.refs_2_, ...), custom_call_target="tpu_custom_call" | custom-call | flops 1 | bytes 1 | tf_op jit(solution)/shard_map/pallas_call | solution.py:64
  258.7 6.1 %shard_map.136 = bf16[1024,1024]{1,0:T(8,128)(2,1)S(1)} custom-call(bf16[1024,8]{1,0:T(8,128)(2,1)S(1)} %convert_bitcast_fusion.1.refs_0_, bf16[1024,8]{1,0:T(8,128)(2,1)S(1)} %convert_bitcast_fusion.refs_1_, bf16[1280,1024]{1,0:T(8,128)(2,1)} %bitcast.17.refs_2_), custom_call_target="tpu_custom_call" | custom-call | flops 1 | bytes 1 | tf_op jit(solution)/shard_map/pallas_call | solution.py:64
  264.9 1.4 copy-done.4
  266.3 5.6 %all-to-all-start.4 = ((bf16[8,80,1024]{2,1,0:T(8,128)(2,1)}), bf16[8,80,1024]{2,1,0:T(8,128)(2,1)}, u32[]{:S(2)}, u32[]{:S(2)}) async-start(bf16[8,80,1024]{2,1,0:T(8,128)(2,1)} %bitcast.64), calls=%async_computation.6 | async-start | bytes 2621440 | tf_op jit(solution)/shard_map/all_to_all | solution.py:249
  272.6 1.3 collective-permute-start.7
  274.7 15.2 %all-to-all-done.4 = bf16[8,80,1024]{2,1,0:T(8,128)(2,1)} async-done(((bf16[8,80,1024]{2,1,0:T(8,128)(2,1)}), bf16[8,80,1024]{2,1,0:T(8,128)(2,1)}, u32[]{:S(2)}, u32[]{:S(2)}) %all-to-all-start.4) | async-done | bytes 1310752 | tf_op jit(solution)/shard_map/all_to_all | solution.py:249
  289.9 2.7 shard_map.137
  292.6 1.0 copy-done.9
  294.3 0.9 collective-permute-start.9
  295.3 1.7 collective-permute-start.13
  297.0 5.9 %shard_map.138 = (bf16[640,1024]{1,0:T(8,128)(2,1)}, bf16[640,1536]{1,0:T(8,128)(2,1)}) custom-call(s32[1]{0:T(128)} %bitcast.5.x_ref, bf16[160,1536]{1,0:T(8,128)(2,1)} %get-tuple-element.38.refs_0_, bf16[160,1536]{1,0:T(8,128)(2,1)} %collective-permute-done.7.refs_1_, bf16[160,1536]{1,0:T(8,128)(2,1)} %collective-permute-done.8.refs_2_, ...), custom_call_target="tpu_custom_call" | custom-call | flops 1 | bytes 1 | tf_op jit(solution)/shard_map/pallas_call | solution.py:64
  302.9 5.8 %all-to-all-start.5 = ((bf16[8,80,1024]{2,1,0:T(8,128)(2,1)}), bf16[8,80,1024]{2,1,0:T(8,128)(2,1)}, u32[]{:S(2)}, u32[]{:S(2)}) async-start(bf16[8,80,1024]{2,1,0:T(8,128)(2,1)} %bitcast.65), calls=%async_computation.7 | async-start | bytes 2621440 | tf_op jit(solution)/shard_map/all_to_all | solution.py:249
  308.7 1.1 add_convert_fusion.6
  309.9 2.7 collective-permute-start.14
  312.7 6.3 %collective-permute-done.10 = bf16[128,1024]{1,0:T(8,128)(2,1)S(1)} collective-permute-done((bf16[128,1024]{1,0:T(8,128)(2,1)S(1)}, bf16[128,1024]{1,0:T(8,128)(2,1)S(1)}, u32[]{:S(2)}, u32[]{:S(2)}) %collective-permute-start.10) | collective-permute-done | bytes 262176 | tf_op jit(solution)/shard_map/ppermute | solution.py:25
  319.0 1.0 add_convert_fusion.4
  320.3 1.5 copy-done.6
  321.8 1.5 copy-done.7
  323.3 4.2 %shard_map.139 = bf16[1024,768]{1,0:T(8,128)(2,1)} custom-call(bf16[8,160,1024]{2,1,0:T(8,128)(2,1)S(1)} %all_to_all.30.near_ref.far_ref, bf16[8,160,1024]{2,1,0:T(8,128)(2,1)S(1)} %all_to_all.30.near_ref.far_ref, bf16[640,1536]{1,0:T(8,128)(2,1)S(1)} %copy-done.7, bf16[640,1536]{1,0:T(8,128)(2,1)S(1)} %copy-done.6), custom_call_target="tpu_custom_call" | custom-call | flops 1 | bytes 1 | tf_op jit(solution)/shard_map/pallas_call | solution.py:64
  327.5 4.2 %shard_map.140 = bf16[1024,768]{1,0:T(8,128)(2,1)} custom-call(bf16[8,160,1024]{2,1,0:T(8,128)(2,1)S(1)} %all_to_all.30.near_ref.far_ref, bf16[8,160,1024]{2,1,0:T(8,128)(2,1)S(1)} %all_to_all.30.near_ref.far_ref, bf16[640,1536]{1,0:T(8,128)(2,1)S(1)} %copy-done.7, bf16[640,1536]{1,0:T(8,128)(2,1)S(1)} %copy-done.6), custom_call_target="tpu_custom_call" | custom-call | flops 1 | bytes 1 | tf_op jit(solution)/shard_map/pallas_call | solution.py:64
  331.8 2.8 shard_map.141
  334.6 1.1 add_convert_fusion.3
  335.8 2.7 collective-permute-start.15
  338.5 4.5 %collective-permute-done.15 = bf16[128,1024]{1,0:T(8,128)(2,1)S(1)} collective-permute-done((bf16[128,1024]{1,0:T(8,128)(2,1)S(1)}, bf16[128,1024]{1,0:T(8,128)(2,1)S(1)}, u32[]{:S(2)}, u32[]{:S(2)}) %collective-permute-start.15) | collective-permute-done | bytes 262176 | tf_op jit(solution)/shard_map/ppermute | solution.py:25
  343.1 3.5 collective-permute-start.16
  346.5 5.3 %shard_map.142 = bf16[768,1024]{1,0:T(8,128)(2,1)} custom-call(bf16[1280,768]{1,0:T(8,128)(2,1)S(1)} %copy-done.5, bf16[1280,1024]{1,0:T(8,128)(2,1)} %bitcast.12.rows_ref.right_ref), custom_call_target="tpu_custom_call" | custom-call | flops 1 | bytes 1 | tf_op jit(solution)/shard_map/pallas_call | solution.py:64
  351.9 0.8 add_convert_fusion
  (94 shorter events, 8.0 us)
Async XLA Ops:
  7.2 43.9 %all-gather.4.cloned.1.call-start = ((), (), s32[]{:S(2)}) async-start(), calls=%async_computation.8 | async-start | bytes 2359296 | tf_op jit(solution)/shard_map/all_gather | solution.py:252
  9.9 16.3 %all-to-all-start = ((f32[8,16,128]{2,1,0:T(8,128)}), f32[8,16,128]{2,1,0:T(8,128)S(1)}, u32[]{:S(2)}, u32[]{:S(2)}) async-start(f32[8,16,128]{2,1,0:T(8,128)} %broadcast_in_dim.52), calls=%async_computation | async-start | bytes 131072 | tf_op jit(solution)/shard_map/all_to_all | solution.py:224
  18.9 88.1 %all-gather.6.cloned.1.call-start = ((), (), s32[]{:S(2)}) async-start(), calls=%async_computation.9 | async-start | bytes 2359296 | tf_op jit(solution)/shard_map/all_gather | solution.py:262
  26.7 24.4 %copy-start.16 = (f32[8,8,128]{0,2,1:T(8,128)}, f32[8,8,128]{0,2,1:T(8,128)S(1)}, u32[]{:S(2)}) copy-start(f32[8,8,128]{0,2,1:T(8,128)S(1)} %copy.27) | copy-start | bytes 98308
  26.8 24.4 %copy-start.20 = (s32[8,1024]{0,1:T(8,128)}, s32[8,1024]{0,1:T(8,128)S(1)}, u32[]{:S(2)}) copy-start(s32[8,1024]{0,1:T(8,128)S(1)} %bitcast_convert_fusion) | copy-start | bytes 98308
  51.1 108.2 %reduce-scatter.3.cloned.1.call-start = ((), (), s32[]{:S(2)}) async-start(), calls=%async_computation.10 | async-start | bytes 4915200 | tf_op jit(solution)/shard_map/reduce_scatter | solution.py:280
  51.3 1.6 copy-start.11
  55.8 40.9 %copy-start.1 = (bf16[1,1024,768]{2,1,0:T(8,128)(2,1)S(1)}, bf16[1,1024,768]{2,1,0:T(8,128)(2,1)}, u32[]{:S(2)}) copy-start(bf16[1,1024,768]{2,1,0:T(8,128)(2,1)} %param.13) | copy-start | bytes 4718596
  55.8 40.9 %copy-start.2 = (bf16[1,1024,768]{2,1,0:T(8,128)(2,1)S(1)}, bf16[1,1024,768]{2,1,0:T(8,128)(2,1)}, u32[]{:S(2)}) copy-start(bf16[1,1024,768]{2,1,0:T(8,128)(2,1)} %param.14) | copy-start | bytes 4718596
  102.5 2.0 copy-start
  104.9 0.8 copy-start.18
  107.0 1.6 copy-start.12
  111.9 1.6 copy-start.3
  113.5 37.4 %all-to-all-start.2 = ((bf16[8,160,1024]{2,1,0:T(8,128)(2,1)}), bf16[8,160,1024]{2,1,0:T(8,128)(2,1)}, u32[]{:S(2)}, u32[]{:S(2)}) async-start(bf16[8,160,1024]{2,1,0:T(8,128)(2,1)} %bitcast.52), calls=%async_computation.2 | async-start | bytes 5242880 | tf_op jit(solution)/shard_map/all_to_all | solution.py:249
  118.8 84.7 %all-gather.8.cloned.1.call-start = ((), (), s32[]{:S(2)}) async-start(), calls=%async_computation.11 | async-start | bytes 2457600 | tf_op jit(solution)/shard_map/all_gather | solution.py:294
  150.9 1.4 copy-start.8
  156.9 0.8 copy-start.13
  157.7 0.8 copy-start.14
  158.5 0.8 copy-start.15
  159.2 1.2 copy-start.10
  161.6 13.5 %collective-permute-start = (bf16[320,768]{1,0:T(8,128)(2,1)}, bf16[320,768]{1,0:T(8,128)(2,1)}, u32[]{:S(2)}, u32[]{:S(2)}) collective-permute-start(bf16[320,768]{1,0:T(8,128)(2,1)} %copy-done.15), channel_id=1, source_target_pairs={{0,1},{1,2},{2,3},{3,0},{4,5},{5,6},{6,7},{7,4},{8,9},{9,10},{10,1... | collective-permute-start | bytes 1474568 | tf_op jit(solution)/shard_map/ppermute | solution.py:25
  162.8 34.4 %collective-permute-start.1 = (bf16[320,768]{1,0:T(8,128)(2,1)}, bf16[320,768]{1,0:T(8,128)(2,1)}, u32[]{:S(2)}, u32[]{:S(2)}) collective-permute-start(bf16[320,768]{1,0:T(8,128)(2,1)} %copy-done.14), channel_id=1, source_target_pairs={{0,2},{1,3},{2,0},{3,1},{4,6},{5,7},{6,4},{7,5},{8,10},{9,11},{10,... | collective-permute-start | bytes 1474568 | tf_op jit(solution)/shard_map/ppermute | solution.py:25
  165.2 32.0 %collective-permute-start.2 = (bf16[320,768]{1,0:T(8,128)(2,1)S(1)}, bf16[320,768]{1,0:T(8,128)(2,1)}, u32[]{:S(2)}, u32[]{:S(2)}) collective-permute-start(bf16[320,768]{1,0:T(8,128)(2,1)S(1)} %get-tuple-element.35), channel_id=1, source_target_pairs={{0,3},{1,0},{2,1},{3,2},{4,7},{5,4},{6,5},{7,6},{8,11},{9,8},{10,9... | collective-permute-start | bytes 1474568 | tf_op jit(solution)/shard_map/ppermute | solution.py:25
  209.3 49.4 %all-to-all-start.3 = ((bf16[8,160,1024]{2,1,0:T(8,128)(2,1)}), bf16[8,160,1024]{2,1,0:T(8,128)(2,1)}, u32[]{:S(2)}, u32[]{:S(2)}) async-start(bf16[8,160,1024]{2,1,0:T(8,128)(2,1)} %bitcast.58), calls=%async_computation.4 | async-start | bytes 5242880 | tf_op jit(solution)/shard_map/all_to_all | solution.py:249
  214.2 7.8 %copy-start.19 = (f32[8,8,128]{0,2,1:T(8,128)S(1)}, f32[8,8,128]{0,2,1:T(8,128)}, u32[]{:S(2)}) copy-start(f32[8,8,128]{0,2,1:T(8,128)} %copy-done.18) | copy-start | bytes 98308
  214.2 138.5 %reduce-scatter.5.cloned.1.call-start = ((), (), s32[]{:S(2)}) async-start(), calls=%async_computation.12 | async-start | bytes 2359296 | tf_op jit(solution)/shard_map/reduce_scatter | solution.py:333
  217.6 14.2 %collective-permute-start.3 = (bf16[160,1536]{1,0:T(8,128)(2,1)}, bf16[160,1536]{1,0:T(8,128)(2,1)}, u32[]{:S(2)}, u32[]{:S(2)}) collective-permute-start(bf16[160,1536]{1,0:T(8,128)(2,1)} %get-tuple-element.38.refs_0_), channel_id=1, source_target_pairs={{0,1},{1,2},{2,3},{3,0},{4,5},{5,6},{6,7},{7,4},{8,9},{9,10},{10,1... | collective-permute-start | bytes 1474568 | tf_op jit(solution)/shard_map/ppermute | solution.py:25
  218.8 13.0 %collective-permute-start.4 = (bf16[160,1536]{1,0:T(8,128)(2,1)}, bf16[160,1536]{1,0:T(8,128)(2,1)}, u32[]{:S(2)}, u32[]{:S(2)}) collective-permute-start(bf16[160,1536]{1,0:T(8,128)(2,1)} %get-tuple-element.40.refs_0_), channel_id=1, source_target_pairs={{0,3},{1,0},{2,1},{3,2},{4,7},{5,4},{6,5},{7,6},{8,11},{9,8},{10,9... | collective-permute-start | bytes 1474568 | tf_op jit(solution)/shard_map/ppermute | solution.py:25
  220.3 22.9 %collective-permute-start.5 = (bf16[160,1536]{1,0:T(8,128)(2,1)}, bf16[160,1536]{1,0:T(8,128)(2,1)}, u32[]{:S(2)}, u32[]{:S(2)}) collective-permute-start(bf16[160,1536]{1,0:T(8,128)(2,1)} %get-tuple-element.40.refs_0_), channel_id=1, source_target_pairs={{0,2},{1,3},{2,0},{3,1},{4,6},{5,7},{6,4},{7,5},{8,10},{9,11},{10,... | collective-permute-start | bytes 1474568 | tf_op jit(solution)/shard_map/ppermute | solution.py:25
  221.8 31.1 %collective-permute-start.6 = (bf16[160,1536]{1,0:T(8,128)(2,1)}, bf16[160,1536]{1,0:T(8,128)(2,1)}, u32[]{:S(2)}, u32[]{:S(2)}) collective-permute-start(bf16[160,1536]{1,0:T(8,128)(2,1)} %get-tuple-element.40.refs_0_), channel_id=1, source_target_pairs={{0,1},{1,2},{2,3},{3,0},{4,5},{5,6},{6,7},{7,4},{8,9},{9,10},{10,1... | collective-permute-start | bytes 1474568 | tf_op jit(solution)/shard_map/ppermute | solution.py:25
  222.0 36.6 %copy-start.17 = (f32[8,8,128]{0,2,1:T(8,128)S(1)}, f32[8,8,128]{0,2,1:T(8,128)}, u32[]{:S(2)}) copy-start(f32[8,8,128]{0,2,1:T(8,128)} %copy-done.16) | copy-start | bytes 98308
  264.9 1.4 copy-start.4
  266.2 5.6 %copy-start.22 = (s32[8]{0:T(128)S(1)}, s32[8]{0:T(128)}, u32[]{:S(2)}) copy-start(s32[8]{0:T(128)} %constant.108.clone) | copy-start | bytes 100
  266.2 6.3 %copy-start.21 = (bf16[160,1536]{1,0:T(8,128)(2,1)S(1)}, bf16[160,1536]{1,0:T(8,128)(2,1)}, u32[]{:S(2)}) copy-start(bf16[160,1536]{1,0:T(8,128)(2,1)} %get-tuple-element.38.refs_0_) | copy-start | bytes 1474564
  266.3 23.6 %all-to-all-start.4 = ((bf16[8,80,1024]{2,1,0:T(8,128)(2,1)}), bf16[8,80,1024]{2,1,0:T(8,128)(2,1)}, u32[]{:S(2)}, u32[]{:S(2)}) async-start(bf16[8,80,1024]{2,1,0:T(8,128)(2,1)} %bitcast.64), calls=%async_computation.6 | async-start | bytes 2621440 | tf_op jit(solution)/shard_map/all_to_all | solution.py:249
  272.6 24.4 %collective-permute-start.7 = (bf16[160,1536]{1,0:T(8,128)(2,1)S(1)}, bf16[160,1536]{1,0:T(8,128)(2,1)}, u32[]{:S(2)}, u32[]{:S(2)}) collective-permute-start(bf16[160,1536]{1,0:T(8,128)(2,1)S(1)} %copy-done.21), channel_id=1, source_target_pairs={{0,3},{1,0},{2,1},{3,2},{4,7},{5,4},{6,5},{7,6},{8,11},{9,8},{10,9... | collective-permute-start | bytes 1474568 | tf_op jit(solution)/shard_map/ppermute | solution.py:25
  273.8 23.2 %collective-permute-start.8 = (bf16[160,1536]{1,0:T(8,128)(2,1)S(1)}, bf16[160,1536]{1,0:T(8,128)(2,1)}, u32[]{:S(2)}, u32[]{:S(2)}) collective-permute-start(bf16[160,1536]{1,0:T(8,128)(2,1)S(1)} %copy-done.21), channel_id=1, source_target_pairs={{0,2},{1,3},{2,0},{3,1},{4,6},{5,7},{6,4},{7,5},{8,10},{9,11},{10,... | collective-permute-start | bytes 1474568 | tf_op jit(solution)/shard_map/ppermute | solution.py:25
  292.6 1.0 copy-start.9
  294.3 14.3 %collective-permute-start.9 = (bf16[64,1024]{1,0:T(8,128)(2,1)}, bf16[64,1024]{1,0:T(8,128)(2,1)S(1)}, u32[]{:S(2)}, u32[]{:S(2)}) collective-permute-start(bf16[64,1024]{1,0:T(8,128)(2,1)} %get-tuple-element.59), channel_id=1, source_target_pairs={{0,8},{8,16},{16,24},{24,32},{32,40},{40,48},{48,56},{56,0},{1,9},... | collective-permute-start | bytes 393224 | tf_op jit(solution)/shard_map/ppermute | solution.py:25
  295.3 13.4 %collective-permute-start.13 = (bf16[64,1024]{1,0:T(8,128)(2,1)}, bf16[64,1024]{1,0:T(8,128)(2,1)}, u32[]{:S(2)}, u32[]{:S(2)}) collective-permute-start(bf16[64,1024]{1,0:T(8,128)(2,1)} %get-tuple-element.60), channel_id=1, source_target_pairs={{0,56},{8,0},{16,8},{24,16},{32,24},{40,32},{48,40},{56,48},{1,57}... | collective-permute-start | bytes 393224 | tf_op jit(solution)/shard_map/ppermute | solution.py:25
  302.9 28.9 %all-to-all-start.5 = ((bf16[8,80,1024]{2,1,0:T(8,128)(2,1)}), bf16[8,80,1024]{2,1,0:T(8,128)(2,1)}, u32[]{:S(2)}, u32[]{:S(2)}) async-start(bf16[8,80,1024]{2,1,0:T(8,128)(2,1)} %bitcast.65), calls=%async_computation.7 | async-start | bytes 2621440 | tf_op jit(solution)/shard_map/all_to_all | solution.py:249
  309.8 9.2 %collective-permute-start.10 = (bf16[128,1024]{1,0:T(8,128)(2,1)S(1)}, bf16[128,1024]{1,0:T(8,128)(2,1)S(1)}, u32[]{:S(2)}, u32[]{:S(2)}) collective-permute-start(bf16[128,1024]{1,0:T(8,128)(2,1)S(1)} %pad_maximum_fusion), channel_id=1, source_target_pairs={{0,8},{8,16},{16,24},{24,32},{32,40},{40,48},{48,56},{56,0},{1,9},... | collective-permute-start | bytes 786440 | tf_op jit(solution)/shard_map/ppermute | solution.py:25
  309.9 24.7 %collective-permute-start.14 = (bf16[128,1024]{1,0:T(8,128)(2,1)S(1)}, bf16[128,1024]{1,0:T(8,128)(2,1)S(1)}, u32[]{:S(2)}, u32[]{:S(2)}) collective-permute-start(bf16[128,1024]{1,0:T(8,128)(2,1)S(1)} %pad_maximum_fusion.1), channel_id=1, source_target_pairs={{0,56},{8,0},{16,8},{24,16},{32,24},{40,32},{48,40},{56,48},{1,57}... | collective-permute-start | bytes 786440 | tf_op jit(solution)/shard_map/ppermute | solution.py:25
  320.0 14.6 %collective-permute-start.11 = (bf16[128,1024]{1,0:T(8,128)(2,1)S(1)}, bf16[128,1024]{1,0:T(8,128)(2,1)}, u32[]{:S(2)}, u32[]{:S(2)}) collective-permute-start(bf16[128,1024]{1,0:T(8,128)(2,1)S(1)} %add_convert_fusion.4), channel_id=1, source_target_pairs={{0,8},{8,16},{16,24},{24,32},{32,40},{40,48},{48,56},{56,0},{1,9},... | collective-permute-start | bytes 786440 | tf_op jit(solution)/shard_map/ppermute | solution.py:25
  320.2 1.6 copy-start.6
  321.8 1.5 copy-start.7
  331.8 14.8 %copy-start.5 = (bf16[1280,768]{1,0:T(8,128)(2,1)S(1)}, bf16[1280,768]{1,0:T(8,128)(2,1)}, u32[]{:S(2)}) copy-start(bf16[1280,768]{1,0:T(8,128)(2,1)} %all-gather.8.cloned.1.call-done.hidden_ref.left_ref) | copy-start | bytes 5898244
  335.8 7.2 %collective-permute-start.15 = (bf16[128,1024]{1,0:T(8,128)(2,1)S(1)}, bf16[128,1024]{1,0:T(8,128)(2,1)S(1)}, u32[]{:S(2)}, u32[]{:S(2)}) collective-permute-start(bf16[128,1024]{1,0:T(8,128)(2,1)S(1)} %get-tuple-element.56), channel_id=1, source_target_pairs={{0,56},{8,0},{16,8},{24,16},{32,24},{40,32},{48,40},{56,48},{1,57}... | collective-permute-start | bytes 786440 | tf_op jit(solution)/shard_map/ppermute | solution.py:25
  338.5 13.3 %collective-permute-start.12 = (bf16[128,1024]{1,0:T(8,128)(2,1)S(1)}, bf16[128,1024]{1,0:T(8,128)(2,1)S(1)}, u32[]{:S(2)}, u32[]{:S(2)}) collective-permute-start(bf16[128,1024]{1,0:T(8,128)(2,1)S(1)} %get-tuple-element.55), channel_id=1, source_target_pairs={{0,8},{8,16},{16,24},{24,32},{32,40},{40,48},{48,56},{56,0},{1,9},... | collective-permute-start | bytes 786440 | tf_op jit(solution)/shard_map/ppermute | solution.py:25
  343.1 8.8 %collective-permute-start.16 = (bf16[128,1024]{1,0:T(8,128)(2,1)S(1)}, bf16[128,1024]{1,0:T(8,128)(2,1)S(1)}, u32[]{:S(2)}, u32[]{:S(2)}) collective-permute-start(bf16[128,1024]{1,0:T(8,128)(2,1)S(1)} %add_convert_fusion.1), channel_id=1, source_target_pairs={{0,56},{8,0},{16,8},{24,16},{32,24},{40,32},{48,40},{56,48},{1,57}... | collective-permute-start | bytes 786440 | tf_op jit(solution)/shard_map/ppermute | solution.py:25
Sparse Core Ops, SparseCore 0:
  9.8 41.1 all-gather.3
  52.8 39.8 all-gather.5
  104.6 44.4 reduce-scatter.2
  161.7 41.8 all-gather.7
  266.4 38.1 reduce-scatter.4
where the time goes:
time: 361 us; the launch traced here: 359 us
  waiting for transfers between devices  157 us (43%)
  Pallas kernels  63.8 us (18%)
  starting transfers between devices  53.7 us (15%)
  blocking collectives  40.9 us (11%)
  local copies, waits for them, and re-layouts  23.5 us (7%)
  between operations  14.2 us (4%)
  other arithmetic  6.12 us (2%)
    ppermute x17, waiting for transfers between devices, shift(): return lax.ppermute(value, axis, [(i, (i + by) % n) for i in range(n)])  72.4 us
    pallas_call x15, Pallas kernels, call(): pl.pallas_call(body, out_shape=outs, grid_spec=spec, compiler_params=pltp...  63.8 us
    all_to_all x4, waiting for transfers between devices, swap(): lax.all_to_all(rows.reshape(DEST, -1, width), ('y', 'core'), 0, 0, tiled=...  47.3 us
    all_to_all x1, blocking collectives, swap(): lax.all_to_all(rows.reshape(DEST, -1, width), ('y', 'core'), 0, 0, tiled=...  40.9 us
    all_gather x1, waiting for transfers between devices, per_device(): all_tokens = lax.all_gather(tokens, 'z', axis=0, tiled=True)  24.3 us
    ppermute x17, starting transfers between devices, shift(): return lax.ppermute(value, axis, [(i, (i + by) % n) for i in range(n)])  22.9 us
    all_to_all x4, starting transfers between devices, swap(): lax.all_to_all(rows.reshape(DEST, -1, width), ('y', 'core'), 0, 0, tiled=...  21.6 us
    unnamed x46, local copies, waits for them, and re-layouts  18 us
  transfers between devices with their start and end apart: 27, of which 12 were waited for; matrix products, arithmetic and copies ran while one was open for 3% of the time, Pallas kernels for 14%

commit v1 on v0

--- a/solution.py
+++ b/solution.py
@@ -280,6 +280,8 @@
     sums = lax.psum_scatter(sums, "x", scatter_dimension=0, tiled=True)
     grads = swap(picked)
     quarter = struct((QUARTER, hid))
+    sums = after(sums, grads)
+    hidden = call(hidden_body, 1, [sums], [whole(sums)], quarter, whole(quarter))
     pieces = call(
         back_body,
         NX,
@@ -287,10 +289,8 @@
         [turned_rows(grads), whole(down_w)],
         [quarter] * NX,
         [whole(quarter)] * NX,
-        x=x,
-    )
-    sums = after(sums, pieces[0])
-    hidden = call(hidden_body, 1, [sums], [whole(sums)], quarter, whole(quarter))
+        x=after(x, hidden),
+    )
     hidden = lax.all_gather(hidden, "x", axis=0, tiled=True)
     pieces = [pieces[0], shift(pieces[1], "x", 1), shift(pieces[2], "x", 2), shift(pieces[3], "x", -1)]
     out = struct((ROWS, width))
@@ -324,7 +324,7 @@
             vmem=MOST,
         )
 
-    far_input, far = to_input(far, near[3])
+    far_input, far = to_input(far, out_rows)
     far_rows = swap(after(far_input, mixed_rows))
     mixed = mix(after(place, far_input), mixed_rows, weight)
     far_sums = mix(after(far_place, mixed), far_rows)
@@ -333,13 +333,14 @@
     mixed = lax.psum_scatter(mixed, "z", scatter_dimension=0, tiled=True)
     grad_gate = outer_chunks(rows, near, far, tiles, 0)
     grad_up = outer_chunks(rows, near, after(far, grad_gate), tiles, tiles)
-    near_sums = mix(near_place, after(near_rows, grad_up))
+    near_sums = mix(after(near_place, grad_up), near_rows)
     grad_down = outer(after(hidden, near_sums), grads)
 
     at = {o: far_sums[i * tok : (i + 1) * tok] for i, o in enumerate(OFFSETS[NB:])}
     at.update((o, near_sums[i * tok : (i + 1) * tok]) for i, o in enumerate(OFFSETS[:NB]))
     half = tok // 2
     low, high = shift(at[4][:half], "z", 1), shift(at[4][half:], "z", -1)
+    low, high = after(low, grad_up), after(high, grad_up)
     up = shift(jnp.concatenate([plus(at[3][:half], low), at[3][half:]], 0), "z", 1)
     down = shift(jnp.concatenate([at[-3][:half], plus(at[-3][half:], high)], 0), "z", -1)
     for step in (2, 1):

time: 361 us -> 350 us (0.970)
  blocking collectives: 40.9 us -> 77.3 us
  waiting for transfers between devices: 157 us -> 122 us
  starting transfers between devices: 53.7 us -> 44.9 us
    all_to_all x1 -> x2, blocking collectives: 40.9 us -> 77.3 us  [swap(): lax.all_to_all(rows.reshape(DEST, -1, width), ('y', 'core'), 0, 0, tiled=...]
    all_to_all x4 -> x3, waiting for transfers between devices: 47.3 us -> 14 us  [swap(): lax.all_to_all(rows.reshape(DEST, -1, width), ('y', 'core'), 0, 0, tiled=...]
    all_to_all x4 -> x3, starting transfers between devices: 21.6 us -> 16.3 us  [swap(): lax.all_to_all(rows.reshape(DEST, -1, width), ('y', 'core'), 0, 0, tiled=...]
    all_gather x1, waiting for transfers between devices: 6.36 us -> 2.35 us  [per_device(): hidden = lax.all_gather(hidden, 'x', axis=0, tiled=True)]
  transfers between devices with their start and end apart: 27 -> 26, of which waited for: 12 -> 14; matrix products, arithmetic and copies ran while one was open for 3% -> 3% of each run, Pallas kernels for 14% -> 14%
where the time goes in v1:
time: 350 us; the launch traced here: 347 us
  waiting for transfers between devices  122 us (35%)
  blocking collectives  77.3 us (22%)
  Pallas kernels  61 us (17%)
  starting transfers between devices  44.9 us (13%)
  local copies, waits for them, and re-layouts  22 us (6%)
  between operations  14.2 us (4%)
  other arithmetic  5.03 us (1%)
    all_to_all x2, blocking collectives, swap(): lax.all_to_all(rows.reshape(DEST, -1, width), ('y', 'core'), 0, 0, tiled=...  77.3 us
    ppermute x17, waiting for transfers between devices, shift(): return lax.ppermute(value, axis, [(i, (i + by) % n) for i in range(n)])  73.5 us
    pallas_call x15, Pallas kernels, call(): pl.pallas_call(body, out_shape=outs, grid_spec=spec, compiler_params=pltp...  61 us
    all_gather x1, waiting for transfers between devices, per_device(): all_tokens = lax.all_gather(tokens, 'z', axis=0, tiled=True)  24.3 us
    ppermute x17, starting transfers between devices, shift(): return lax.ppermute(value, axis, [(i, (i + by) % n) for i in range(n)])  19.4 us
    unnamed x46, local copies, waits for them, and re-layouts  16.5 us
    all_to_all x3, starting transfers between devices, swap(): lax.all_to_all(rows.reshape(DEST, -1, width), ('y', 'core'), 0, 0, tiled=...  16.3 us
    all_to_all x3, waiting for transfers between devices, swap(): lax.all_to_all(rows.reshape(DEST, -1, width), ('y', 'core'), 0, 0, tiled=...  14 us
  transfers between devices with their start and end apart: 26, of which 14 were waited for; matrix products, arithmetic and copies ran while one was open for 3% of the time, Pallas kernels for 14%

profile of v1, /device:TPU:1, one launch (start us, length us, event | category | flops | bytes accessed | tf_op | source)
XLA Modules:
  0.0 346.7 jit_solution(15002786082104134206)
XLA Ops:
  7.9 0.7 convert_bitcast_fusion.4
  8.6 0.7 pad_maximum_fusion.2
  9.9 9.0 %all-to-all-start = ((f32[8,16,128]{2,1,0:T(8,128)}), f32[8,16,128]{2,1,0:T(8,128)S(1)}, u32[]{:S(2)}, u32[]{:S(2)}) async-start(f32[8,16,128]{2,1,0:T(8,128)} %broadcast_in_dim.52), calls=%async_computation | async-start | bytes 131072 | tf_op jit(solution)/shard_map/all_to_all | solution.py:224
  19.0 1.3 gather_fusion
  20.3 5.8 %all-to-all-done = f32[8,16,128]{2,1,0:T(8,128)S(1)} async-done(((f32[8,16,128]{2,1,0:T(8,128)}), f32[8,16,128]{2,1,0:T(8,128)S(1)}, u32[]{:S(2)}, u32[]{:S(2)}) %all-to-all-start) | async-done | bytes 65568 | tf_op jit(solution)/shard_map/all_to_all | solution.py:224
  26.8 24.3 %all-gather.4.cloned.1.call-done.refs_1_ = bf16[1024,1024]{1,0:T(8,128)(2,1)} async-done(((bf16[128,1024]{1,0:T(8,128)(2,1)}), bf16[1024,1024]{1,0:T(8,128)(2,1)}) %all-gather.4.cloned.1.call-update) | async-done | bytes 2097168 | tf_op jit(solution)/shard_map/all_gather | solution.py:252
  51.3 1.6 copy-done.13
  52.9 2.9 shard_map.128
  55.8 40.9 %all_to_all.30.near_ref.far_ref = bf16[8,160,1024]{2,1,0:T(8,128)(2,1)S(1)} all-to-all(bf16[8,160,1024]{2,1,0:T(8,128)(2,1)S(1)} %bitcast.56), channel_id=1, replica_groups=mesh['y'=4,'z'=8,'core'=2,'x'=4] {'y','core'}, dimensions={0} | all-to-all | bytes 5242880 | tf_op jit(solution)/shard_map/all_to_all | solution.py:249
  96.7 5.8 %shard_map.129 = bf16[1280,1536]{1,0:T(8,128)(2,1)S(1)} custom-call(bf16[1280,1024]{1,0:T(8,128)(2,1)S(1)} %bitcast.46, bf16[1024,768]{1,0:T(8,128)(2,1)S(1)} %bitcast.51, bf16[1024,768]{1,0:T(8,128)(2,1)S(1)} %bitcast.54), custom_call_target="tpu_custom_call" | custom-call | flops 1 | bytes 1 | tf_op jit(solution)/shard_map/pallas_call | solution.py:64
  102.5 1.9 copy-done.2
  105.0 1.2 copy.30.refs_0_
  106.3 1.6 copy-done.14
  107.8 3.3 shard_map.130
  111.1 36.4 %all_to_all.31 = bf16[8,160,1024]{2,1,0:T(8,128)(2,1)} all-to-all(bf16[8,160,1024]{2,1,0:T(8,128)(2,1)S(1)} %bitcast.55), channel_id=1, replica_groups=mesh['y'=4,'z'=8,'core'=2,'x'=4] {'y','core'}, dimensions={0} | all-to-all | bytes 5242880 | tf_op jit(solution)/shard_map/all_to_all | solution.py:249
  147.6 1.5 reduce-scatter.3.cloned.1.call-done.sums_ref
  149.0 1.2 copy-done.12
  150.2 1.1 shard_map.131
  151.4 1.7 copy-done
  153.1 1.4 copy-done.9
  154.5 3.1 shard_map.132
  157.6 0.8 copy-done.15
  158.4 2.1 collective-permute-start.1
  160.5 1.2 collective-permute-start.2
  161.7 14.9 %collective-permute-done.b = bf16[320,768]{1,0:T(8,128)(2,1)S(1)} collective-permute-done((bf16[320,768]{1,0:T(8,128)(2,1)S(1)}, bf16[320,768]{1,0:T(8,128)(2,1)S(1)}, u32[]{:S(2)}, u32[]{:S(2)}) %collective-permute-start) | collective-permute-done | bytes 491552 | tf_op jit(solution)/shard_map/ppermute | solution.py:25
  176.6 17.9 %collective-permute-done.1.c = bf16[320,768]{1,0:T(8,128)(2,1)S(1)} collective-permute-done((bf16[320,768]{1,0:T(8,128)(2,1)S(1)}, bf16[320,768]{1,0:T(8,128)(2,1)S(1)}, u32[]{:S(2)}, u32[]{:S(2)}) %collective-permute-start.1) | collective-permute-done | bytes 491552 | tf_op jit(solution)/shard_map/ppermute | solution.py:25
  194.4 0.8 copy-done.20
  195.2 1.9 collective-permute-done.2.d
  197.1 2.4 all-gather.8.cloned.1.call-done.hidden_ref.left_ref
  199.5 5.8 %shard_map.133 = bf16[1280,1024]{1,0:T(8,128)(2,1)} custom-call(bf16[1280,768]{1,0:T(8,128)(2,1)} %all-gather.8.cloned.1.call-done.hidden_ref.left_ref, bf16[768,1024]{1,0:T(8,128)(2,1)} %bitcast.57), custom_call_target="tpu_custom_call" | custom-call | flops 1 | bytes 1 | tf_op jit(solution)/shard_map/pallas_call | solution.py:64
  205.2 5.1 %all-to-all-start.3 = ((bf16[8,160,1024]{2,1,0:T(8,128)(2,1)}), bf16[8,160,1024]{2,1,0:T(8,128)(2,1)}, u32[]{:S(2)}, u32[]{:S(2)}) async-start(bf16[8,160,1024]{2,1,0:T(8,128)(2,1)} %bitcast.61), calls=%async_computation.4 | async-start | bytes 5242880 | tf_op jit(solution)/shard_map/all_to_all | solution.py:249
  210.3 3.3 shard_map.134
  213.7 0.8 collective-permute-start.5
  214.5 3.0 collective-permute-start.4
  217.5 10.2 %collective-permute-done.5.refs_3_ = bf16[160,1536]{1,0:T(8,128)(2,1)} collective-permute-done((bf16[160,1536]{1,0:T(8,128)(2,1)}, bf16[160,1536]{1,0:T(8,128)(2,1)}, u32[]{:S(2)}, u32[]{:S(2)}) %collective-permute-start.5) | collective-permute-done | bytes 491552 | tf_op jit(solution)/shard_map/ppermute | solution.py:25
  227.7 11.6 %collective-permute-done.4.refs_2_ = bf16[160,1536]{1,0:T(8,128)(2,1)} collective-permute-done((bf16[160,1536]{1,0:T(8,128)(2,1)}, bf16[160,1536]{1,0:T(8,128)(2,1)}, u32[]{:S(2)}, u32[]{:S(2)}) %collective-permute-start.4) | collective-permute-done | bytes 491552 | tf_op jit(solution)/shard_map/ppermute | solution.py:25
  239.3 5.8 %shard_map.135 = (bf16[640,1024]{1,0:T(8,128)(2,1)}, bf16[640,1536]{1,0:T(8,128)(2,1)}) custom-call(s32[1]{0:T(128)} %bitcast.5.x_ref, bf16[160,1536]{1,0:T(8,128)(2,1)} %get-tuple-element.43.refs_0_, bf16[160,1536]{1,0:T(8,128)(2,1)} %collective-permute-done.3.refs_1_, bf16[160,1536]{1,0:T(8,128)(2,1)} %collective-permute-done.4.refs_2_, ...), custom_call_target="tpu_custom_call" | custom-call | flops 1 | bytes 1 | tf_op jit(solution)/shard_map/pallas_call | solution.py:64
  245.2 6.1 %shard_map.136 = bf16[1024,1024]{1,0:T(8,128)(2,1)S(1)} custom-call(bf16[1024,8]{1,0:T(8,128)(2,1)S(1)} %convert_bitcast_fusion.1.refs_0_, bf16[1024,8]{1,0:T(8,128)(2,1)S(1)} %convert_bitcast_fusion.refs_1_, bf16[1280,1024]{1,0:T(8,128)(2,1)} %bitcast.17.refs_2_), custom_call_target="tpu_custom_call" | custom-call | flops 1 | bytes 1 | tf_op jit(solution)/shard_map/pallas_call | solution.py:64
  251.3 1.3 copy-done.5
  252.7 5.7 %all-to-all-start.4 = ((bf16[8,80,1024]{2,1,0:T(8,128)(2,1)}), bf16[8,80,1024]{2,1,0:T(8,128)(2,1)}, u32[]{:S(2)}, u32[]{:S(2)}) async-start(bf16[8,80,1024]{2,1,0:T(8,128)(2,1)} %bitcast.67), calls=%async_computation.6 | async-start | bytes 2621440 | tf_op jit(solution)/shard_map/all_to_all | solution.py:249
  259.6 2.7 collective-permute-start.7
  262.5 14.0 %all-to-all-done.4 = bf16[8,80,1024]{2,1,0:T(8,128)(2,1)} async-done(((bf16[8,80,1024]{2,1,0:T(8,128)(2,1)}), bf16[8,80,1024]{2,1,0:T(8,128)(2,1)}, u32[]{:S(2)}, u32[]{:S(2)}) %all-to-all-start.4) | async-done | bytes 1310752 | tf_op jit(solution)/shard_map/all_to_all | solution.py:249
  276.5 2.7 shard_map.137
  279.2 1.0 copy-done.10
  280.2 0.7 fusion.14
  280.9 3.0 collective-permute-start.13
  284.3 5.9 %shard_map.138 = (bf16[640,1024]{1,0:T(8,128)(2,1)}, bf16[640,1536]{1,0:T(8,128)(2,1)}) custom-call(s32[1]{0:T(128)} %bitcast.5.x_ref, bf16[160,1536]{1,0:T(8,128)(2,1)} %get-tuple-element.49.refs_0_, bf16[160,1536]{1,0:T(8,128)(2,1)} %collective-permute-done.6.refs_1_, bf16[160,1536]{1,0:T(8,128)(2,1)} %collective-permute-done.7.refs_2_, ...), custom_call_target="tpu_custom_call" | custom-call | flops 1 | bytes 1 | tf_op jit(solution)/shard_map/pallas_call | solution.py:64
  290.2 5.5 %all-to-all-start.5 = ((bf16[8,80,1024]{2,1,0:T(8,128)(2,1)}), bf16[8,80,1024]{2,1,0:T(8,128)(2,1)}, u32[]{:S(2)}, u32[]{:S(2)}) async-start(bf16[8,80,1024]{2,1,0:T(8,128)(2,1)} %bitcast.68), calls=%async_computation.7 | async-start | bytes 2621440 | tf_op jit(solution)/shard_map/all_to_all | solution.py:249
  295.6 1.5 copy-done.7
  297.2 1.5 copy-done.8
  298.7 4.2 %shard_map.139 = bf16[1024,768]{1,0:T(8,128)(2,1)} custom-call(bf16[8,160,1024]{2,1,0:T(8,128)(2,1)S(1)} %all_to_all.30.near_ref.far_ref, bf16[8,160,1024]{2,1,0:T(8,128)(2,1)S(1)} %all_to_all.30.near_ref.far_ref, bf16[640,1536]{1,0:T(8,128)(2,1)S(1)} %copy-done.8, bf16[640,1536]{1,0:T(8,128)(2,1)S(1)} %copy-done.7), custom_call_target="tpu_custom_call" | custom-call | flops 1 | bytes 1 | tf_op jit(solution)/shard_map/pallas_call | solution.py:64
  302.9 4.2 %shard_map.140 = bf16[1024,768]{1,0:T(8,128)(2,1)} custom-call(bf16[8,160,1024]{2,1,0:T(8,128)(2,1)S(1)} %all_to_all.30.near_ref.far_ref, bf16[8,160,1024]{2,1,0:T(8,128)(2,1)S(1)} %all_to_all.30.near_ref.far_ref, bf16[640,1536]{1,0:T(8,128)(2,1)S(1)} %copy-done.8, bf16[640,1536]{1,0:T(8,128)(2,1)S(1)} %copy-done.7), custom_call_target="tpu_custom_call" | custom-call | flops 1 | bytes 1 | tf_op jit(solution)/shard_map/pallas_call | solution.py:64
  307.2 1.0 add_convert_fusion.6
  308.2 1.4 collective-permute-start.10
  309.5 1.9 collective-permute-start.14
  311.4 6.5 %collective-permute-done.10 = bf16[128,1024]{1,0:T(8,128)(2,1)S(1)} collective-permute-done((bf16[128,1024]{1,0:T(8,128)(2,1)S(1)}, bf16[128,1024]{1,0:T(8,128)(2,1)S(1)}, u32[]{:S(2)}, u32[]{:S(2)}) %collective-permute-start.10) | collective-permute-done | bytes 262176 | tf_op jit(solution)/shard_map/ppermute | solution.py:25
  318.2 2.9 shard_map.141
  321.1 5.4 %collective-permute-done.11 = bf16[128,1024]{1,0:T(8,128)(2,1)} collective-permute-done((bf16[128,1024]{1,0:T(8,128)(2,1)S(1)}, bf16[128,1024]{1,0:T(8,128)(2,1)}, u32[]{:S(2)}, u32[]{:S(2)}) %collective-permute-start.11) | collective-permute-done | bytes 262176 | tf_op jit(solution)/shard_map/ppermute | solution.py:25
  326.5 1.1 add_convert_fusion.3
  327.8 1.5 collective-permute-start.12
  329.2 4.8 %collective-permute-done.15 = bf16[128,1024]{1,0:T(8,128)(2,1)S(1)} collective-permute-done((bf16[128,1024]{1,0:T(8,128)(2,1)S(1)}, bf16[128,1024]{1,0:T(8,128)(2,1)S(1)}, u32[]{:S(2)}, u32[]{:S(2)}) %collective-permute-start.15) | collective-permute-done | bytes 262176 | tf_op jit(solution)/shard_map/ppermute | solution.py:25
  334.1 1.2 collective-permute-start.16
  335.3 4.0 %shard_map.142 = bf16[768,1024]{1,0:T(8,128)(2,1)} custom-call(bf16[1280,768]{1,0:T(8,128)(2,1)S(1)} %copy-done.6, bf16[1280,1024]{1,0:T(8,128)(2,1)S(1)} %bitcast.48), custom_call_target="tpu_custom_call" | custom-call | flops 1 | bytes 1 | tf_op jit(solution)/shard_map/pallas_call | solution.py:64
  339.4 0.8 add_convert_fusion
  (93 shorter events, 5.1 us)
Async XLA Ops:
  7.2 43.9 %all-gather.4.cloned.1.call-start = ((), (), s32[]{:S(2)}) async-start(), calls=%async_computation.8 | async-start | bytes 2359296 | tf_op jit(solution)/shard_map/all_gather | solution.py:252
  9.9 16.3 %all-to-all-start = ((f32[8,16,128]{2,1,0:T(8,128)}), f32[8,16,128]{2,1,0:T(8,128)S(1)}, u32[]{:S(2)}, u32[]{:S(2)}) async-start(f32[8,16,128]{2,1,0:T(8,128)} %broadcast_in_dim.52), calls=%async_computation | async-start | bytes 131072 | tf_op jit(solution)/shard_map/all_to_all | solution.py:224
  18.9 87.3 %all-gather.6.cloned.1.call-start = ((), (), s32[]{:S(2)}) async-start(), calls=%async_computation.10 | async-start | bytes 2359296 | tf_op jit(solution)/shard_map/all_gather | solution.py:262
  26.7 29.1 %copy-start.16 = (f32[8,8,128]{0,2,1:T(8,128)}, f32[8,8,128]{0,2,1:T(8,128)S(1)}, u32[]{:S(2)}) copy-start(f32[8,8,128]{0,2,1:T(8,128)S(1)} %copy.27) | copy-start | bytes 98308
  26.8 29.0 %copy-start.18 = (s32[8,1024]{0,1:T(8,128)}, s32[8,1024]{0,1:T(8,128)S(1)}, u32[]{:S(2)}) copy-start(s32[8,1024]{0,1:T(8,128)S(1)} %bitcast_convert_fusion) | copy-start | bytes 98308
  51.1 98.0 %reduce-scatter.3.cloned.1.call-start = ((), (), s32[]{:S(2)}) async-start(), calls=%async_computation.9 | async-start | bytes 4915200 | tf_op jit(solution)/shard_map/reduce_scatter | solution.py:280
  51.3 1.6 copy-start.13
  55.8 40.9 %copy-start.3 = (bf16[1,1024,768]{2,1,0:T(8,128)(2,1)S(1)}, bf16[1,1024,768]{2,1,0:T(8,128)(2,1)}, u32[]{:S(2)}) copy-start(bf16[1,1024,768]{2,1,0:T(8,128)(2,1)} %param.13) | copy-start | bytes 4718596
  55.8 40.9 %copy-start.4 = (bf16[1,1024,768]{2,1,0:T(8,128)(2,1)S(1)}, bf16[1,1024,768]{2,1,0:T(8,128)(2,1)}, u32[]{:S(2)}) copy-start(bf16[1,1024,768]{2,1,0:T(8,128)(2,1)} %param.14) | copy-start | bytes 4718596
  102.5 1.9 copy-start.2
  104.5 95.0 %all-gather.8.cloned.1.call-start = ((), (), s32[]{:S(2)}) async-start(), calls=%async_computation.11 | async-start | bytes 2457600 | tf_op jit(solution)/shard_map/all_gather | solution.py:294
  106.2 1.6 copy-start.14
  149.0 1.2 copy-start.12
  151.3 1.7 copy-start
  153.1 1.4 copy-start.9
  157.6 0.8 copy-start.15
  158.4 18.2 %collective-permute-start = (bf16[320,768]{1,0:T(8,128)(2,1)S(1)}, bf16[320,768]{1,0:T(8,128)(2,1)S(1)}, u32[]{:S(2)}, u32[]{:S(2)}) collective-permute-start(bf16[320,768]{1,0:T(8,128)(2,1)S(1)} %get-tuple-element.37), channel_id=1, source_target_pairs={{0,1},{1,2},{2,3},{3,0},{4,5},{5,6},{6,7},{7,4},{8,9},{9,10},{10,1... | collective-permute-start | bytes 1474568 | tf_op jit(solution)/shard_map/ppermute | solution.py:25
  158.4 36.1 %collective-permute-start.1 = (bf16[320,768]{1,0:T(8,128)(2,1)S(1)}, bf16[320,768]{1,0:T(8,128)(2,1)S(1)}, u32[]{:S(2)}, u32[]{:S(2)}) collective-permute-start(bf16[320,768]{1,0:T(8,128)(2,1)S(1)} %get-tuple-element.38), channel_id=1, source_target_pairs={{0,2},{1,3},{2,0},{3,1},{4,6},{5,7},{6,4},{7,5},{8,10},{9,11},{10,... | collective-permute-start | bytes 1474568 | tf_op jit(solution)/shard_map/ppermute | solution.py:25
  160.5 36.6 %collective-permute-start.2 = (bf16[320,768]{1,0:T(8,128)(2,1)S(1)}, bf16[320,768]{1,0:T(8,128)(2,1)}, u32[]{:S(2)}, u32[]{:S(2)}) collective-permute-start(bf16[320,768]{1,0:T(8,128)(2,1)S(1)} %get-tuple-element.39), channel_id=1, source_target_pairs={{0,3},{1,0},{2,1},{3,2},{4,7},{5,4},{6,5},{7,6},{8,11},{9,8},{10,9... | collective-permute-start | bytes 1474568 | tf_op jit(solution)/shard_map/ppermute | solution.py:25
  176.6 17.9 %copy-start.19 = (bf16[320,768]{1,0:T(8,128)(2,1)}, bf16[320,768]{1,0:T(8,128)(2,1)S(1)}, u32[]{:S(2)}) copy-start(bf16[320,768]{1,0:T(8,128)(2,1)S(1)} %collective-permute-done.b) | copy-start | bytes 1474564
  194.4 0.8 copy-start.20
  205.2 40.0 %all-to-all-start.3 = ((bf16[8,160,1024]{2,1,0:T(8,128)(2,1)}), bf16[8,160,1024]{2,1,0:T(8,128)(2,1)}, u32[]{:S(2)}, u32[]{:S(2)}) async-start(bf16[8,160,1024]{2,1,0:T(8,128)(2,1)} %bitcast.61), calls=%async_computation.4 | async-start | bytes 5242880 | tf_op jit(solution)/shard_map/all_to_all | solution.py:249
  210.3 129.9 %reduce-scatter.5.cloned.1.call-start = ((), (), s32[]{:S(2)}) async-start(), calls=%async_computation.12 | async-start | bytes 2359296 | tf_op jit(solution)/shard_map/reduce_scatter | solution.py:333
  213.7 14.0 %collective-permute-start.5 = (bf16[160,1536]{1,0:T(8,128)(2,1)}, bf16[160,1536]{1,0:T(8,128)(2,1)}, u32[]{:S(2)}, u32[]{:S(2)}) collective-permute-start(bf16[160,1536]{1,0:T(8,128)(2,1)} %get-tuple-element.43.refs_0_), channel_id=1, source_target_pairs={{0,1},{1,2},{2,3},{3,0},{4,5},{5,6},{6,7},{7,4},{8,9},{9,10},{10,1... | collective-permute-start | bytes 1474568 | tf_op jit(solution)/shard_map/ppermute | solution.py:25
  214.5 24.8 %collective-permute-start.4 = (bf16[160,1536]{1,0:T(8,128)(2,1)}, bf16[160,1536]{1,0:T(8,128)(2,1)}, u32[]{:S(2)}, u32[]{:S(2)}) collective-permute-start(bf16[160,1536]{1,0:T(8,128)(2,1)} %get-tuple-element.43.refs_0_), channel_id=1, source_target_pairs={{0,2},{1,3},{2,0},{3,1},{4,6},{5,7},{6,4},{7,5},{8,10},{9,11},{10,... | collective-permute-start | bytes 1474568 | tf_op jit(solution)/shard_map/ppermute | solution.py:25
  217.5 21.9 %collective-permute-start.3 = (bf16[160,1536]{1,0:T(8,128)(2,1)}, bf16[160,1536]{1,0:T(8,128)(2,1)}, u32[]{:S(2)}, u32[]{:S(2)}) collective-permute-start(bf16[160,1536]{1,0:T(8,128)(2,1)} %get-tuple-element.43.refs_0_), channel_id=1, source_target_pairs={{0,3},{1,0},{2,1},{3,2},{4,7},{5,4},{6,5},{7,6},{8,11},{9,8},{10,9... | collective-permute-start | bytes 1474568 | tf_op jit(solution)/shard_map/ppermute | solution.py:25
  217.5 27.7 %copy-start.17 = (f32[8,8,128]{0,2,1:T(8,128)S(1)}, f32[8,8,128]{0,2,1:T(8,128)}, u32[]{:S(2)}) copy-start(f32[8,8,128]{0,2,1:T(8,128)} %copy-done.16) | copy-start | bytes 98308
  251.3 1.3 copy-start.5
  252.7 5.8 %copy-start.22 = (s32[8]{0:T(128)S(1)}, s32[8]{0:T(128)}, u32[]{:S(2)}) copy-start(s32[8]{0:T(128)} %constant.108.clone) | copy-start | bytes 100
  252.7 6.5 %copy-start.21 = (bf16[160,1536]{1,0:T(8,128)(2,1)S(1)}, bf16[160,1536]{1,0:T(8,128)(2,1)}, u32[]{:S(2)}) copy-start(bf16[160,1536]{1,0:T(8,128)(2,1)} %get-tuple-element.49.refs_0_) | copy-start | bytes 1474564
  252.7 23.8 %all-to-all-start.4 = ((bf16[8,80,1024]{2,1,0:T(8,128)(2,1)}), bf16[8,80,1024]{2,1,0:T(8,128)(2,1)}, u32[]{:S(2)}, u32[]{:S(2)}) async-start(bf16[8,80,1024]{2,1,0:T(8,128)(2,1)} %bitcast.67), calls=%async_computation.6 | async-start | bytes 2621440 | tf_op jit(solution)/shard_map/all_to_all | solution.py:249
  259.2 24.8 %collective-permute-start.8 = (bf16[160,1536]{1,0:T(8,128)(2,1)S(1)}, bf16[160,1536]{1,0:T(8,128)(2,1)}, u32[]{:S(2)}, u32[]{:S(2)}) collective-permute-start(bf16[160,1536]{1,0:T(8,128)(2,1)S(1)} %copy-done.21), channel_id=1, source_target_pairs={{0,1},{1,2},{2,3},{3,0},{4,5},{5,6},{6,7},{7,4},{8,9},{9,10},{10,1... | collective-permute-start | bytes 1474568 | tf_op jit(solution)/shard_map/ppermute | solution.py:25
  259.6 24.7 %collective-permute-start.7 = (bf16[160,1536]{1,0:T(8,128)(2,1)S(1)}, bf16[160,1536]{1,0:T(8,128)(2,1)}, u32[]{:S(2)}, u32[]{:S(2)}) collective-permute-start(bf16[160,1536]{1,0:T(8,128)(2,1)S(1)} %copy-done.21), channel_id=1, source_target_pairs={{0,2},{1,3},{2,0},{3,1},{4,6},{5,7},{6,4},{7,5},{8,10},{9,11},{10,... | collective-permute-start | bytes 1474568 | tf_op jit(solution)/shard_map/ppermute | solution.py:25
  262.3 22.0 %collective-permute-start.6 = (bf16[160,1536]{1,0:T(8,128)(2,1)S(1)}, bf16[160,1536]{1,0:T(8,128)(2,1)}, u32[]{:S(2)}, u32[]{:S(2)}) collective-permute-start(bf16[160,1536]{1,0:T(8,128)(2,1)S(1)} %copy-done.21), channel_id=1, source_target_pairs={{0,3},{1,0},{2,1},{3,2},{4,7},{5,4},{6,5},{7,6},{8,11},{9,8},{10,9... | collective-permute-start | bytes 1474568 | tf_op jit(solution)/shard_map/ppermute | solution.py:25
  279.2 1.0 copy-start.10
  280.9 26.2 %collective-permute-start.13 = (bf16[64,1024]{1,0:T(8,128)(2,1)}, bf16[64,1024]{1,0:T(8,128)(2,1)S(1)}, u32[]{:S(2)}, u32[]{:S(2)}) collective-permute-start(bf16[64,1024]{1,0:T(8,128)(2,1)} %get-tuple-element.66), channel_id=1, source_target_pairs={{0,56},{8,0},{16,8},{24,16},{32,24},{40,32},{48,40},{56,48},{1,57}... | collective-permute-start | bytes 393224 | tf_op jit(solution)/shard_map/ppermute | solution.py:25
  283.9 23.2 %collective-permute-start.9 = (bf16[64,1024]{1,0:T(8,128)(2,1)}, bf16[64,1024]{1,0:T(8,128)(2,1)}, u32[]{:S(2)}, u32[]{:S(2)}) collective-permute-start(bf16[64,1024]{1,0:T(8,128)(2,1)} %get-tuple-element.65), channel_id=1, source_target_pairs={{0,8},{8,16},{16,24},{24,32},{32,40},{40,48},{48,56},{56,0},{1,9},... | collective-permute-start | bytes 393224 | tf_op jit(solution)/shard_map/ppermute | solution.py:25
  290.2 28.0 %all-to-all-start.5 = ((bf16[8,80,1024]{2,1,0:T(8,128)(2,1)}), bf16[8,80,1024]{2,1,0:T(8,128)(2,1)}, u32[]{:S(2)}, u32[]{:S(2)}) async-start(bf16[8,80,1024]{2,1,0:T(8,128)(2,1)} %bitcast.68), calls=%async_computation.7 | async-start | bytes 2621440 | tf_op jit(solution)/shard_map/all_to_all | solution.py:249
  295.6 1.5 copy-start.7
  297.2 1.5 copy-start.8
  302.9 4.2 %copy-start.11 = (bf16[512,1024]{1,0:T(8,128)(2,1)S(1)}, bf16[512,1024]{1,0:T(8,128)(2,1)}, u32[]{:S(2)}) copy-start(bf16[512,1024]{1,0:T(8,128)(2,1)} %copy-done.10) | copy-start | bytes 3145732
  308.2 9.7 %collective-permute-start.10 = (bf16[128,1024]{1,0:T(8,128)(2,1)S(1)}, bf16[128,1024]{1,0:T(8,128)(2,1)S(1)}, u32[]{:S(2)}, u32[]{:S(2)}) collective-permute-start(bf16[128,1024]{1,0:T(8,128)(2,1)S(1)} %pad_maximum_fusion), channel_id=1, source_target_pairs={{0,8},{8,16},{16,24},{24,32},{32,40},{40,48},{48,56},{56,0},{1,9},... | collective-permute-start | bytes 786440 | tf_op jit(solution)/shard_map/ppermute | solution.py:25
  309.5 11.6 %collective-permute-start.14 = (bf16[128,1024]{1,0:T(8,128)(2,1)S(1)}, bf16[128,1024]{1,0:T(8,128)(2,1)S(1)}, u32[]{:S(2)}, u32[]{:S(2)}) collective-permute-start(bf16[128,1024]{1,0:T(8,128)(2,1)S(1)} %pad_maximum_fusion.1), channel_id=1, source_target_pairs={{0,56},{8,0},{16,8},{24,16},{32,24},{40,32},{48,40},{56,48},{1,57}... | collective-permute-start | bytes 786440 | tf_op jit(solution)/shard_map/ppermute | solution.py:25
  317.9 8.6 %collective-permute-start.11 = (bf16[128,1024]{1,0:T(8,128)(2,1)S(1)}, bf16[128,1024]{1,0:T(8,128)(2,1)}, u32[]{:S(2)}, u32[]{:S(2)}) collective-permute-start(bf16[128,1024]{1,0:T(8,128)(2,1)S(1)} %add_convert_fusion.4), channel_id=1, source_target_pairs={{0,8},{8,16},{16,24},{24,32},{32,40},{40,48},{48,56},{56,0},{1,9},... | collective-permute-start | bytes 786440 | tf_op jit(solution)/shard_map/ppermute | solution.py:25
  318.2 17.1 %copy-start.1 = (bf16[8,160,1024]{2,1,0:T(8,128)(2,1)S(1)}, bf16[8,160,1024]{2,1,0:T(8,128)(2,1)}, u32[]{:S(2)}) copy-start(bf16[8,160,1024]{2,1,0:T(8,128)(2,1)} %all_to_all.31) | copy-start | bytes 7864324
  318.2 17.1 %copy-start.6 = (bf16[1280,768]{1,0:T(8,128)(2,1)S(1)}, bf16[1280,768]{1,0:T(8,128)(2,1)}, u32[]{:S(2)}) copy-start(bf16[1280,768]{1,0:T(8,128)(2,1)} %all-gather.8.cloned.1.call-done.hidden_ref.left_ref) | copy-start | bytes 5898244
  327.7 6.3 %collective-permute-start.15 = (bf16[128,1024]{1,0:T(8,128)(2,1)S(1)}, bf16[128,1024]{1,0:T(8,128)(2,1)S(1)}, u32[]{:S(2)}, u32[]{:S(2)}) collective-permute-start(bf16[128,1024]{1,0:T(8,128)(2,1)S(1)} %get-tuple-element.62), channel_id=1, source_target_pairs={{0,56},{8,0},{16,8},{24,16},{32,24},{40,32},{48,40},{56,48},{1,57}... | collective-permute-start | bytes 786440 | tf_op jit(solution)/shard_map/ppermute | solution.py:25
  327.8 11.6 %collective-permute-start.12 = (bf16[128,1024]{1,0:T(8,128)(2,1)S(1)}, bf16[128,1024]{1,0:T(8,128)(2,1)S(1)}, u32[]{:S(2)}, u32[]{:S(2)}) collective-permute-start(bf16[128,1024]{1,0:T(8,128)(2,1)S(1)} %get-tuple-element.61), channel_id=1, source_target_pairs={{0,8},{8,16},{16,24},{24,32},{32,40},{40,48},{48,56},{56,0},{1,9},... | collective-permute-start | bytes 786440 | tf_op jit(solution)/shard_map/ppermute | solution.py:25
  334.1 5.3 %collective-permute-start.16 = (bf16[128,1024]{1,0:T(8,128)(2,1)S(1)}, bf16[128,1024]{1,0:T(8,128)(2,1)S(1)}, u32[]{:S(2)}, u32[]{:S(2)}) collective-permute-start(bf16[128,1024]{1,0:T(8,128)(2,1)S(1)} %add_convert_fusion.1), channel_id=1, source_target_pairs={{0,56},{8,0},{16,8},{24,16},{32,24},{40,32},{48,40},{56,48},{1,57}... | collective-permute-start | bytes 786440 | tf_op jit(solution)/shard_map/ppermute | solution.py:25
Sparse Core Ops, SparseCore 0:
  9.8 41.1 all-gather.3
  52.8 39.8 all-gather.5
  104.6 44.4 reduce-scatter.2
  151.5 47.9 all-gather.7
  252.8 41.2 reduce-scatter.4

commit v2 on v1

--- a/solution.py
+++ b/solution.py
@@ -321,7 +321,6 @@
             [out, both],
             [whole(out), whole(both)],
             x=after(x, turn),
-            vmem=MOST,
         )
 
     far_input, far = to_input(far, out_rows)

time: 350 us -> 353 us (level)
  local copies, waits for them, and re-layouts: 22 us -> 29.8 us
  Pallas kernels: 61 us -> 55.3 us
    unnamed x46 -> x64, local copies, waits for them, and re-layouts: 16.5 us -> 24.1 us
    pallas_call x15, Pallas kernels: 61 us -> 55.3 us  [call(): pl.pallas_call(body, out_shape=outs, grid_spec=spec, compiler_params=pltp...]
  transfers between devices with their start and end apart: 26 -> 26, of which waited for: 14 -> 14; matrix products, arithmetic and copies ran while one was open for 3% -> 3% of each run, Pallas kernels for 14% -> 12%
where the time goes in v2:
time: 353 us; the launch traced here: 349 us
  waiting for transfers between devices  123 us (35%)
  blocking collectives  77.3 us (22%)
  Pallas kernels  55.3 us (16%)
  starting transfers between devices  44.7 us (13%)
  local copies, waits for them, and re-layouts  29.8 us (8%)
  between operations  14.2 us (4%)
  other arithmetic  5.03 us (1%)
    all_to_all x2, blocking collectives, swap(): lax.all_to_all(rows.reshape(DEST, -1, width), ('y', 'core'), 0, 0, tiled=...  77.3 us
    ppermute x17, waiting for transfers between devices, shift(): return lax.ppermute(value, axis, [(i, (i + by) % n) for i in range(n)])  74.3 us
    pallas_call x15, Pallas kernels, call(): pl.pallas_call(body, out_shape=outs, grid_spec=spec, compiler_params=pltp...  55.3 us
    all_gather x1, waiting for transfers between devices, per_device(): all_tokens = lax.all_gather(tokens, 'z', axis=0, tiled=True)  24.3 us
    unnamed x64, local copies, waits for them, and re-layouts  24.1 us
    ppermute x17, starting transfers between devices, shift(): return lax.ppermute(value, axis, [(i, (i + by) % n) for i in range(n)])  19.4 us
    all_to_all x3, starting transfers between devices, swap(): lax.all_to_all(rows.reshape(DEST, -1, width), ('y', 'core'), 0, 0, tiled=...  16.2 us
    all_to_all x3, waiting for transfers between devices, swap(): lax.all_to_all(rows.reshape(DEST, -1, width), ('y', 'core'), 0, 0, tiled=...  14 us
  transfers between devices with their start and end apart: 26, of which 14 were waited for; matrix products, arithmetic and copies ran while one was open for 3% of the time, Pallas kernels for 12%

profile of v2, /device:TPU:1, one launch (start us, length us, event | category | flops | bytes accessed | tf_op | source)
XLA Modules:
  0.0 349.4 jit_solution(16509231399902563516)
XLA Ops:
  9.9 9.0 %all-to-all-start = ((f32[8,16,128]{2,1,0:T(8,128)}), f32[8,16,128]{2,1,0:T(8,128)S(1)}, u32[]{:S(2)}, u32[]{:S(2)}) async-start(f32[8,16,128]{2,1,0:T(8,128)} %broadcast_in_dim.52), calls=%async_computation | async-start | bytes 131072 | tf_op jit(solution)/shard_map/all_to_all | solution.py:224
  19.0 1.3 gather_fusion
  20.3 5.8 %all-to-all-done = f32[8,16,128]{2,1,0:T(8,128)S(1)} async-done(((f32[8,16,128]{2,1,0:T(8,128)}), f32[8,16,128]{2,1,0:T(8,128)S(1)}, u32[]{:S(2)}, u32[]{:S(2)}) %all-to-all-start) | async-done | bytes 65568 | tf_op jit(solution)/shard_map/all_to_all | solution.py:224
  26.8 24.3 %all-gather.4.cloned.1.call-done.refs_1_ = bf16[1024,1024]{1,0:T(8,128)(2,1)} async-done(((bf16[128,1024]{1,0:T(8,128)(2,1)}), bf16[1024,1024]{1,0:T(8,128)(2,1)}) %all-gather.4.cloned.1.call-update) | async-done | bytes 2097168 | tf_op jit(solution)/shard_map/all_gather | solution.py:252
  51.3 1.6 copy-done.19
  52.9 2.9 shard_map.128
  55.8 40.9 %all_to_all.30.near_ref.far_ref = bf16[8,160,1024]{2,1,0:T(8,128)(2,1)S(1)} all-to-all(bf16[8,160,1024]{2,1,0:T(8,128)(2,1)S(1)} %bitcast.56), channel_id=1, replica_groups=mesh['y'=4,'z'=8,'core'=2,'x'=4] {'y','core'}, dimensions={0} | all-to-all | bytes 5242880 | tf_op jit(solution)/shard_map/all_to_all | solution.py:249
  96.7 5.8 %shard_map.129 = bf16[1280,1536]{1,0:T(8,128)(2,1)S(1)} custom-call(bf16[1280,1024]{1,0:T(8,128)(2,1)S(1)} %bitcast.46, bf16[1024,768]{1,0:T(8,128)(2,1)S(1)} %bitcast.49, bf16[1024,768]{1,0:T(8,128)(2,1)S(1)} %bitcast.52), custom_call_target="tpu_custom_call" | custom-call | flops 1 | bytes 1 | tf_op jit(solution)/shard_map/pallas_call | solution.py:64
  102.5 1.9 copy-done.2
  105.0 1.2 copy.30.refs_0_
  106.2 1.6 copy-done.20
  107.8 3.3 shard_map.130
  111.1 36.4 %all_to_all.31 = bf16[8,160,1024]{2,1,0:T(8,128)(2,1)} all-to-all(bf16[8,160,1024]{2,1,0:T(8,128)(2,1)S(1)} %bitcast.55), channel_id=1, replica_groups=mesh['y'=4,'z'=8,'core'=2,'x'=4] {'y','core'}, dimensions={0} | all-to-all | bytes 5242880 | tf_op jit(solution)/shard_map/all_to_all | solution.py:249
  147.5 1.5 reduce-scatter.3.cloned.1.call-done.sums_ref
  149.0 1.2 copy-done.18
  150.2 1.1 shard_map.131
  151.3 1.7 copy-done
  153.1 1.4 copy-done.15
  154.5 3.1 shard_map.132
  158.3 2.1 collective-permute-start.1
  160.4 1.2 collective-permute-start.2
  161.6 15.0 %collective-permute-done.b = bf16[320,768]{1,0:T(8,128)(2,1)S(1)} collective-permute-done((bf16[320,768]{1,0:T(8,128)(2,1)S(1)}, bf16[320,768]{1,0:T(8,128)(2,1)S(1)}, u32[]{:S(2)}, u32[]{:S(2)}) %collective-permute-start) | collective-permute-done | bytes 491552 | tf_op jit(solution)/shard_map/ppermute | solution.py:25
  176.6 17.8 %collective-permute-done.1.c = bf16[320,768]{1,0:T(8,128)(2,1)S(1)} collective-permute-done((bf16[320,768]{1,0:T(8,128)(2,1)S(1)}, bf16[320,768]{1,0:T(8,128)(2,1)S(1)}, u32[]{:S(2)}, u32[]{:S(2)}) %collective-permute-start.1) | collective-permute-done | bytes 491552 | tf_op jit(solution)/shard_map/ppermute | solution.py:25
  195.2 2.0 collective-permute-done.2.d
  197.2 2.3 all-gather.8.cloned.1.call-done.hidden_ref.left_ref
  199.5 5.8 %shard_map.133 = bf16[1280,1024]{1,0:T(8,128)(2,1)} custom-call(bf16[1280,768]{1,0:T(8,128)(2,1)} %all-gather.8.cloned.1.call-done.hidden_ref.left_ref, bf16[768,1024]{1,0:T(8,128)(2,1)} %bitcast.57), custom_call_target="tpu_custom_call" | custom-call | flops 1 | bytes 1 | tf_op jit(solution)/shard_map/pallas_call | solution.py:64
  205.2 5.1 %all-to-all-start.3 = ((bf16[8,160,1024]{2,1,0:T(8,128)(2,1)}), bf16[8,160,1024]{2,1,0:T(8,128)(2,1)}, u32[]{:S(2)}, u32[]{:S(2)}) async-start(bf16[8,160,1024]{2,1,0:T(8,128)(2,1)} %bitcast.63), calls=%async_computation.4 | async-start | bytes 5242880 | tf_op jit(solution)/shard_map/all_to_all | solution.py:249
  210.3 3.3 shard_map.134
  214.4 3.0 collective-permute-start.4
  217.5 10.2 %collective-permute-done.5.refs_3_ = bf16[160,1536]{1,0:T(8,128)(2,1)S(1)} collective-permute-done((bf16[160,1536]{1,0:T(8,128)(2,1)}, bf16[160,1536]{1,0:T(8,128)(2,1)S(1)}, u32[]{:S(2)}, u32[]{:S(2)}) %collective-permute-start.5) | collective-permute-done | bytes 491552 | tf_op jit(solution)/shard_map/ppermute | solution.py:25
  227.6 11.7 %collective-permute-done.4.refs_2_ = bf16[160,1536]{1,0:T(8,128)(2,1)S(1)} collective-permute-done((bf16[160,1536]{1,0:T(8,128)(2,1)}, bf16[160,1536]{1,0:T(8,128)(2,1)S(1)}, u32[]{:S(2)}, u32[]{:S(2)}) %collective-permute-start.4) | collective-permute-done | bytes 491552 | tf_op jit(solution)/shard_map/ppermute | solution.py:25
  239.3 1.4 copy-done.4
  240.7 1.4 copy-done.7
  242.1 1.0 copy-done.25
  243.1 2.2 shard_map.135
  245.4 1.3 copy-done.11
  246.7 1.1 copy-done.21
  247.8 6.1 %shard_map.136 = bf16[1024,1024]{1,0:T(8,128)(2,1)S(1)} custom-call(bf16[1024,8]{1,0:T(8,128)(2,1)S(1)} %convert_bitcast_fusion.1.refs_0_, bf16[1024,8]{1,0:T(8,128)(2,1)S(1)} %convert_bitcast_fusion.refs_1_, bf16[1280,1024]{1,0:T(8,128)(2,1)} %bitcast.17.refs_2_), custom_call_target="tpu_custom_call" | custom-call | flops 1 | bytes 1 | tf_op jit(solution)/shard_map/pallas_call | solution.py:64
  254.0 1.3 copy-done.9
  255.3 5.7 %all-to-all-start.4 = ((bf16[8,80,1024]{2,1,0:T(8,128)(2,1)}), bf16[8,80,1024]{2,1,0:T(8,128)(2,1)}, u32[]{:S(2)}, u32[]{:S(2)}) async-start(bf16[8,80,1024]{2,1,0:T(8,128)(2,1)} %bitcast.59), calls=%async_computation.6 | async-start | bytes 2621440 | tf_op jit(solution)/shard_map/all_to_all | solution.py:249
  262.1 2.7 collective-permute-start.7
  265.0 14.0 %all-to-all-done.4 = bf16[8,80,1024]{2,1,0:T(8,128)(2,1)} async-done(((bf16[8,80,1024]{2,1,0:T(8,128)(2,1)}), bf16[8,80,1024]{2,1,0:T(8,128)(2,1)}, u32[]{:S(2)}, u32[]{:S(2)}) %all-to-all-start.4) | async-done | bytes 1310752 | tf_op jit(solution)/shard_map/all_to_all | solution.py:249
  279.0 2.9 shard_map.137
  282.7 3.1 collective-permute-start.13
  285.8 1.0 collective-permute-done.7.refs_2_
  286.8 3.6 %shard_map.138 = (bf16[640,1024]{1,0:T(8,128)(2,1)S(1)}, bf16[640,1536]{1,0:T(8,128)(2,1)S(1)}) custom-call(s32[1]{0:T(128)} %bitcast.5.x_ref, bf16[160,1536]{1,0:T(8,128)(2,1)S(1)} %copy-done.24, bf16[160,1536]{1,0:T(8,128)(2,1)} %collective-permute-done.6.refs_1_, bf16[160,1536]{1,0:T(8,128)(2,1)} %collective-permute-done.7.refs_2_, ...), custom_call_target="tpu_custom_call" | custom-call | flops 1 | bytes 1 | tf_op jit(solution)/shard_map/pallas_call | solution.py:64
  290.4 1.4 copy-done.13
  291.8 1.1 copy-done.22
  292.8 5.5 %all-to-all-start.5 = ((bf16[8,80,1024]{2,1,0:T(8,128)(2,1)}), bf16[8,80,1024]{2,1,0:T(8,128)(2,1)}, u32[]{:S(2)}, u32[]{:S(2)}) async-start(bf16[8,80,1024]{2,1,0:T(8,128)(2,1)} %bitcast.60), calls=%async_computation.7 | async-start | bytes 2621440 | tf_op jit(solution)/shard_map/all_to_all | solution.py:249
  298.3 1.5 copy-done.12
  299.9 1.5 copy-done.14
  301.4 4.2 %shard_map.139 = bf16[1024,768]{1,0:T(8,128)(2,1)} custom-call(bf16[8,160,1024]{2,1,0:T(8,128)(2,1)S(1)} %all_to_all.30.near_ref.far_ref, bf16[8,160,1024]{2,1,0:T(8,128)(2,1)S(1)} %all_to_all.30.near_ref.far_ref, bf16[640,1536]{1,0:T(8,128)(2,1)S(1)} %copy-done.14, bf16[640,1536]{1,0:T(8,128)(2,1)S(1)} %copy-done.12), custom_call_target="tpu_custom_call" | custom-call | flops 1 | bytes 1 | tf_op jit(solution)/shard_map/pallas_call | solution.py:64
  305.6 4.2 %shard_map.140 = bf16[1024,768]{1,0:T(8,128)(2,1)} custom-call(bf16[8,160,1024]{2,1,0:T(8,128)(2,1)S(1)} %all_to_all.30.near_ref.far_ref, bf16[8,160,1024]{2,1,0:T(8,128)(2,1)S(1)} %all_to_all.30.near_ref.far_ref, bf16[640,1536]{1,0:T(8,128)(2,1)S(1)} %copy-done.14, bf16[640,1536]{1,0:T(8,128)(2,1)S(1)} %copy-done.12), custom_call_target="tpu_custom_call" | custom-call | flops 1 | bytes 1 | tf_op jit(solution)/shard_map/pallas_call | solution.py:64
  309.8 1.0 add_convert_fusion.6
  310.8 1.4 collective-permute-start.10
  312.2 1.9 collective-permute-start.14
  314.1 6.5 %collective-permute-done.10 = bf16[128,1024]{1,0:T(8,128)(2,1)S(1)} collective-permute-done((bf16[128,1024]{1,0:T(8,128)(2,1)S(1)}, bf16[128,1024]{1,0:T(8,128)(2,1)S(1)}, u32[]{:S(2)}, u32[]{:S(2)}) %collective-permute-start.10) | collective-permute-done | bytes 262176 | tf_op jit(solution)/shard_map/ppermute | solution.py:25
  320.9 2.9 shard_map.141
  323.8 5.4 %collective-permute-done.11 = bf16[128,1024]{1,0:T(8,128)(2,1)} collective-permute-done((bf16[128,1024]{1,0:T(8,128)(2,1)S(1)}, bf16[128,1024]{1,0:T(8,128)(2,1)}, u32[]{:S(2)}, u32[]{:S(2)}) %collective-permute-start.11) | collective-permute-done | bytes 262176 | tf_op jit(solution)/shard_map/ppermute | solution.py:25
  329.2 1.1 add_convert_fusion.3
  330.5 1.5 collective-permute-start.12
  331.9 4.8 %collective-permute-done.15 = bf16[128,1024]{1,0:T(8,128)(2,1)S(1)} collective-permute-done((bf16[128,1024]{1,0:T(8,128)(2,1)S(1)}, bf16[128,1024]{1,0:T(8,128)(2,1)S(1)}, u32[]{:S(2)}, u32[]{:S(2)}) %collective-permute-start.15) | collective-permute-done | bytes 262176 | tf_op jit(solution)/shard_map/ppermute | solution.py:25
  336.8 1.2 collective-permute-start.16
  338.0 4.0 %shard_map.142 = bf16[768,1024]{1,0:T(8,128)(2,1)} custom-call(bf16[1280,768]{1,0:T(8,128)(2,1)S(1)} %copy-done.10, bf16[1280,1024]{1,0:T(8,128)(2,1)S(1)} %bitcast.48), custom_call_target="tpu_custom_call" | custom-call | flops 1 | bytes 1 | tf_op jit(solution)/shard_map/pallas_call | solution.py:64
  (111 shorter events, 10.2 us)
Async XLA Ops:
  7.2 43.9 %all-gather.4.cloned.1.call-start = ((), (), s32[]{:S(2)}) async-start(), calls=%async_computation.8 | async-start | bytes 2359296 | tf_op jit(solution)/shard_map/all_gather | solution.py:252
  9.9 16.3 %all-to-all-start = ((f32[8,16,128]{2,1,0:T(8,128)}), f32[8,16,128]{2,1,0:T(8,128)S(1)}, u32[]{:S(2)}, u32[]{:S(2)}) async-start(f32[8,16,128]{2,1,0:T(8,128)} %broadcast_in_dim.52), calls=%async_computation | async-start | bytes 131072 | tf_op jit(solution)/shard_map/all_to_all | solution.py:224
  18.9 87.3 %all-gather.6.cloned.1.call-start = ((), (), s32[]{:S(2)}) async-start(), calls=%async_computation.10 | async-start | bytes 2359296 | tf_op jit(solution)/shard_map/all_gather | solution.py:262
  26.7 29.1 %copy-start.26 = (f32[8,8,128]{0,2,1:T(8,128)}, f32[8,8,128]{0,2,1:T(8,128)S(1)}, u32[]{:S(2)}) copy-start(f32[8,8,128]{0,2,1:T(8,128)S(1)} %copy.27) | copy-start | bytes 98308
  26.8 24.4 %copy-start.28 = (s32[8,1024]{0,1:T(8,128)}, s32[8,1024]{0,1:T(8,128)S(1)}, u32[]{:S(2)}) copy-start(s32[8,1024]{0,1:T(8,128)S(1)} %bitcast_convert_fusion) | copy-start | bytes 98308
  51.1 97.9 %reduce-scatter.3.cloned.1.call-start = ((), (), s32[]{:S(2)}) async-start(), calls=%async_computation.9 | async-start | bytes 4915200 | tf_op jit(solution)/shard_map/reduce_scatter | solution.py:280
  51.3 1.6 copy-start.19
  55.8 40.9 %copy-start.3 = (bf16[1,1024,768]{2,1,0:T(8,128)(2,1)S(1)}, bf16[1,1024,768]{2,1,0:T(8,128)(2,1)}, u32[]{:S(2)}) copy-start(bf16[1,1024,768]{2,1,0:T(8,128)(2,1)} %param.13) | copy-start | bytes 4718596
  55.8 40.9 %copy-start.6 = (bf16[1,1024,768]{2,1,0:T(8,128)(2,1)S(1)}, bf16[1,1024,768]{2,1,0:T(8,128)(2,1)}, u32[]{:S(2)}) copy-start(bf16[1,1024,768]{2,1,0:T(8,128)(2,1)} %param.14) | copy-start | bytes 4718596
  102.5 1.9 copy-start.2
  104.4 95.0 %all-gather.8.cloned.1.call-start = ((), (), s32[]{:S(2)}) async-start(), calls=%async_computation.11 | async-start | bytes 2457600 | tf_op jit(solution)/shard_map/all_gather | solution.py:294
  106.2 1.6 copy-start.20
  149.0 1.2 copy-start.18
  151.3 1.7 copy-start
  153.1 1.4 copy-start.15
  157.6 0.8 copy-start.23
  158.3 18.2 %collective-permute-start = (bf16[320,768]{1,0:T(8,128)(2,1)S(1)}, bf16[320,768]{1,0:T(8,128)(2,1)S(1)}, u32[]{:S(2)}, u32[]{:S(2)}) collective-permute-start(bf16[320,768]{1,0:T(8,128)(2,1)S(1)} %get-tuple-element.37), channel_id=1, source_target_pairs={{0,1},{1,2},{2,3},{3,0},{4,5},{5,6},{6,7},{7,4},{8,9},{9,10},{10,1... | collective-permute-start | bytes 1474568 | tf_op jit(solution)/shard_map/ppermute | solution.py:25
  158.3 36.0 %collective-permute-start.1 = (bf16[320,768]{1,0:T(8,128)(2,1)S(1)}, bf16[320,768]{1,0:T(8,128)(2,1)S(1)}, u32[]{:S(2)}, u32[]{:S(2)}) collective-permute-start(bf16[320,768]{1,0:T(8,128)(2,1)S(1)} %get-tuple-element.38), channel_id=1, source_target_pairs={{0,2},{1,3},{2,0},{3,1},{4,6},{5,7},{6,4},{7,5},{8,10},{9,11},{10,... | collective-permute-start | bytes 1474568 | tf_op jit(solution)/shard_map/ppermute | solution.py:25
  160.4 36.7 %collective-permute-start.2 = (bf16[320,768]{1,0:T(8,128)(2,1)S(1)}, bf16[320,768]{1,0:T(8,128)(2,1)}, u32[]{:S(2)}, u32[]{:S(2)}) collective-permute-start(bf16[320,768]{1,0:T(8,128)(2,1)S(1)} %get-tuple-element.39), channel_id=1, source_target_pairs={{0,3},{1,0},{2,1},{3,2},{4,7},{5,4},{6,5},{7,6},{8,11},{9,8},{10,9... | collective-permute-start | bytes 1474568 | tf_op jit(solution)/shard_map/ppermute | solution.py:25
  176.6 17.8 %copy-start.29 = (bf16[320,768]{1,0:T(8,128)(2,1)}, bf16[320,768]{1,0:T(8,128)(2,1)S(1)}, u32[]{:S(2)}) copy-start(bf16[320,768]{1,0:T(8,128)(2,1)S(1)} %collective-permute-done.b) | copy-start | bytes 1474564
  194.4 0.8 copy-start.30
  205.2 42.6 %all-to-all-start.3 = ((bf16[8,160,1024]{2,1,0:T(8,128)(2,1)}), bf16[8,160,1024]{2,1,0:T(8,128)(2,1)}, u32[]{:S(2)}, u32[]{:S(2)}) async-start(bf16[8,160,1024]{2,1,0:T(8,128)(2,1)} %bitcast.63), calls=%async_computation.4 | async-start | bytes 5242880 | tf_op jit(solution)/shard_map/all_to_all | solution.py:249
  210.3 132.6 %reduce-scatter.5.cloned.1.call-start = ((), (), s32[]{:S(2)}) async-start(), calls=%async_computation.12 | async-start | bytes 2359296 | tf_op jit(solution)/shard_map/reduce_scatter | solution.py:332
  213.6 14.0 %collective-permute-start.5 = (bf16[160,1536]{1,0:T(8,128)(2,1)}, bf16[160,1536]{1,0:T(8,128)(2,1)S(1)}, u32[]{:S(2)}, u32[]{:S(2)}) collective-permute-start(bf16[160,1536]{1,0:T(8,128)(2,1)} %get-tuple-element.43.refs_0_), channel_id=1, source_target_pairs={{0,1},{1,2},{2,3},{3,0},{4,5},{5,6},{6,7},{7,4},{8,9},{9,10},{10,1... | collective-permute-start | bytes 1474568 | tf_op jit(solution)/shard_map/ppermute | solution.py:25
  214.4 24.8 %collective-permute-start.4 = (bf16[160,1536]{1,0:T(8,128)(2,1)}, bf16[160,1536]{1,0:T(8,128)(2,1)S(1)}, u32[]{:S(2)}, u32[]{:S(2)}) collective-permute-start(bf16[160,1536]{1,0:T(8,128)(2,1)} %get-tuple-element.43.refs_0_), channel_id=1, source_target_pairs={{0,2},{1,3},{2,0},{3,1},{4,6},{5,7},{6,4},{7,5},{8,10},{9,11},{10,... | collective-permute-start | bytes 1474568 | tf_op jit(solution)/shard_map/ppermute | solution.py:25
  217.4 21.8 %collective-permute-start.3 = (bf16[160,1536]{1,0:T(8,128)(2,1)}, bf16[160,1536]{1,0:T(8,128)(2,1)S(1)}, u32[]{:S(2)}, u32[]{:S(2)}) collective-permute-start(bf16[160,1536]{1,0:T(8,128)(2,1)} %get-tuple-element.43.refs_0_), channel_id=1, source_target_pairs={{0,3},{1,0},{2,1},{3,2},{4,7},{5,4},{6,5},{7,6},{8,11},{9,8},{10,9... | collective-permute-start | bytes 1474568 | tf_op jit(solution)/shard_map/ppermute | solution.py:25
  217.4 30.3 %copy-start.27 = (f32[8,8,128]{0,2,1:T(8,128)S(1)}, f32[8,8,128]{0,2,1:T(8,128)}, u32[]{:S(2)}) copy-start(f32[8,8,128]{0,2,1:T(8,128)} %copy-done.26) | copy-start | bytes 98308
  239.3 1.4 copy-start.4
  240.7 1.4 copy-start.7
  242.1 1.0 copy-start.25
  245.4 1.3 copy-start.11
  246.7 1.1 copy-start.21
  253.9 1.3 copy-start.9
  255.3 5.7 %copy-start.31 = (s32[8]{0:T(128)S(1)}, s32[8]{0:T(128)}, u32[]{:S(2)}) copy-start(s32[8]{0:T(128)} %constant.108.clone) | copy-start | bytes 100
  255.3 6.4 %copy-start.24 = (bf16[160,1536]{1,0:T(8,128)(2,1)S(1)}, bf16[160,1536]{1,0:T(8,128)(2,1)}, u32[]{:S(2)}) copy-start(bf16[160,1536]{1,0:T(8,128)(2,1)} %get-tuple-element.49.refs_0_) | copy-start | bytes 1474564
  255.3 23.7 %all-to-all-start.4 = ((bf16[8,80,1024]{2,1,0:T(8,128)(2,1)}), bf16[8,80,1024]{2,1,0:T(8,128)(2,1)}, u32[]{:S(2)}, u32[]{:S(2)}) async-start(bf16[8,80,1024]{2,1,0:T(8,128)(2,1)} %bitcast.59), calls=%async_computation.6 | async-start | bytes 2621440 | tf_op jit(solution)/shard_map/all_to_all | solution.py:249
  261.7 24.1 %collective-permute-start.8 = (bf16[160,1536]{1,0:T(8,128)(2,1)S(1)}, bf16[160,1536]{1,0:T(8,128)(2,1)}, u32[]{:S(2)}, u32[]{:S(2)}) collective-permute-start(bf16[160,1536]{1,0:T(8,128)(2,1)S(1)} %copy-done.24), channel_id=1, source_target_pairs={{0,1},{1,2},{2,3},{3,0},{4,5},{5,6},{6,7},{7,4},{8,9},{9,10},{10,1... | collective-permute-start | bytes 1474568 | tf_op jit(solution)/shard_map/ppermute | solution.py:25
  262.1 24.7 %collective-permute-start.7 = (bf16[160,1536]{1,0:T(8,128)(2,1)S(1)}, bf16[160,1536]{1,0:T(8,128)(2,1)}, u32[]{:S(2)}, u32[]{:S(2)}) collective-permute-start(bf16[160,1536]{1,0:T(8,128)(2,1)S(1)} %copy-done.24), channel_id=1, source_target_pairs={{0,2},{1,3},{2,0},{3,1},{4,6},{5,7},{6,4},{7,5},{8,10},{9,11},{10,... | collective-permute-start | bytes 1474568 | tf_op jit(solution)/shard_map/ppermute | solution.py:25
  264.8 22.0 %collective-permute-start.6 = (bf16[160,1536]{1,0:T(8,128)(2,1)S(1)}, bf16[160,1536]{1,0:T(8,128)(2,1)}, u32[]{:S(2)}, u32[]{:S(2)}) collective-permute-start(bf16[160,1536]{1,0:T(8,128)(2,1)S(1)} %copy-done.24), channel_id=1, source_target_pairs={{0,3},{1,0},{2,1},{3,2},{4,7},{5,4},{6,5},{7,6},{8,11},{9,8},{10,9... | collective-permute-start | bytes 1474568 | tf_op jit(solution)/shard_map/ppermute | solution.py:25
  279.0 7.8 %copy-start.5 = (bf16[1,1024,768]{2,1,0:T(8,128)(2,1)S(1)}, bf16[1,1024,768]{2,1,0:T(8,128)(2,1)}, u32[]{:S(2)}) copy-start(bf16[1,1024,768]{2,1,0:T(8,128)(2,1)} %param.13) | copy-start | bytes 4718596
  279.0 7.8 %copy-start.8 = (bf16[1,1024,768]{2,1,0:T(8,128)(2,1)S(1)}, bf16[1,1024,768]{2,1,0:T(8,128)(2,1)}, u32[]{:S(2)}) copy-start(bf16[1,1024,768]{2,1,0:T(8,128)(2,1)} %param.14) | copy-start | bytes 4718596
  281.9 5.0 %copy-start.16 = (bf16[512,1024]{1,0:T(8,128)(2,1)}, bf16[512,1024]{1,0:T(8,128)(2,1)S(1)}, u32[]{:S(2)}) copy-start(bf16[512,1024]{1,0:T(8,128)(2,1)S(1)} %shard_map.137) | copy-start | bytes 3145732
  282.7 27.1 %collective-permute-start.13 = (bf16[64,1024]{1,0:T(8,128)(2,1)}, bf16[64,1024]{1,0:T(8,128)(2,1)S(1)}, u32[]{:S(2)}, u32[]{:S(2)}) collective-permute-start(bf16[64,1024]{1,0:T(8,128)(2,1)} %get-tuple-element.66), channel_id=1, source_target_pairs={{0,56},{8,0},{16,8},{24,16},{32,24},{40,32},{48,40},{56,48},{1,57}... | collective-permute-start | bytes 393224 | tf_op jit(solution)/shard_map/ppermute | solution.py:25
  285.8 24.1 %collective-permute-start.9 = (bf16[64,1024]{1,0:T(8,128)(2,1)}, bf16[64,1024]{1,0:T(8,128)(2,1)}, u32[]{:S(2)}, u32[]{:S(2)}) collective-permute-start(bf16[64,1024]{1,0:T(8,128)(2,1)} %get-tuple-element.65), channel_id=1, source_target_pairs={{0,8},{8,16},{16,24},{24,32},{32,40},{40,48},{48,56},{56,0},{1,9},... | collective-permute-start | bytes 393224 | tf_op jit(solution)/shard_map/ppermute | solution.py:25
  290.4 1.4 copy-start.13
  291.8 1.1 copy-start.22
  292.8 28.1 %all-to-all-start.5 = ((bf16[8,80,1024]{2,1,0:T(8,128)(2,1)}), bf16[8,80,1024]{2,1,0:T(8,128)(2,1)}, u32[]{:S(2)}, u32[]{:S(2)}) async-start(bf16[8,80,1024]{2,1,0:T(8,128)(2,1)} %bitcast.60), calls=%async_computation.7 | async-start | bytes 2621440 | tf_op jit(solution)/shard_map/all_to_all | solution.py:249
  298.3 1.5 copy-start.12
  299.9 1.5 copy-start.14
  305.6 4.2 %copy-start.17 = (bf16[512,1024]{1,0:T(8,128)(2,1)S(1)}, bf16[512,1024]{1,0:T(8,128)(2,1)}, u32[]{:S(2)}) copy-start(bf16[512,1024]{1,0:T(8,128)(2,1)} %copy-done.16) | copy-start | bytes 3145732
  310.8 9.7 %collective-permute-start.10 = (bf16[128,1024]{1,0:T(8,128)(2,1)S(1)}, bf16[128,1024]{1,0:T(8,128)(2,1)S(1)}, u32[]{:S(2)}, u32[]{:S(2)}) collective-permute-start(bf16[128,1024]{1,0:T(8,128)(2,1)S(1)} %pad_maximum_fusion), channel_id=1, source_target_pairs={{0,8},{8,16},{16,24},{24,32},{32,40},{40,48},{48,56},{56,0},{1,9},... | collective-permute-start | bytes 786440 | tf_op jit(solution)/shard_map/ppermute | solution.py:25
  312.2 11.6 %collective-permute-start.14 = (bf16[128,1024]{1,0:T(8,128)(2,1)S(1)}, bf16[128,1024]{1,0:T(8,128)(2,1)S(1)}, u32[]{:S(2)}, u32[]{:S(2)}) collective-permute-start(bf16[128,1024]{1,0:T(8,128)(2,1)S(1)} %pad_maximum_fusion.1), channel_id=1, source_target_pairs={{0,56},{8,0},{16,8},{24,16},{32,24},{40,32},{48,40},{56,48},{1,57}... | collective-permute-start | bytes 786440 | tf_op jit(solution)/shard_map/ppermute | solution.py:25
  320.6 8.6 %collective-permute-start.11 = (bf16[128,1024]{1,0:T(8,128)(2,1)S(1)}, bf16[128,1024]{1,0:T(8,128)(2,1)}, u32[]{:S(2)}, u32[]{:S(2)}) collective-permute-start(bf16[128,1024]{1,0:T(8,128)(2,1)S(1)} %add_convert_fusion.4), channel_id=1, source_target_pairs={{0,8},{8,16},{16,24},{24,32},{32,40},{40,48},{48,56},{56,0},{1,9},... | collective-permute-start | bytes 786440 | tf_op jit(solution)/shard_map/ppermute | solution.py:25
  320.9 17.1 %copy-start.1 = (bf16[8,160,1024]{2,1,0:T(8,128)(2,1)S(1)}, bf16[8,160,1024]{2,1,0:T(8,128)(2,1)}, u32[]{:S(2)}) copy-start(bf16[8,160,1024]{2,1,0:T(8,128)(2,1)} %all_to_all.31) | copy-start | bytes 7864324
  320.9 17.1 %copy-start.10 = (bf16[1280,768]{1,0:T(8,128)(2,1)S(1)}, bf16[1280,768]{1,0:T(8,128)(2,1)}, u32[]{:S(2)}) copy-start(bf16[1280,768]{1,0:T(8,128)(2,1)} %all-gather.8.cloned.1.call-done.hidden_ref.left_ref) | copy-start | bytes 5898244
  330.4 6.3 %collective-permute-start.15 = (bf16[128,1024]{1,0:T(8,128)(2,1)S(1)}, bf16[128,1024]{1,0:T(8,128)(2,1)S(1)}, u32[]{:S(2)}, u32[]{:S(2)}) collective-permute-start(bf16[128,1024]{1,0:T(8,128)(2,1)S(1)} %get-tuple-element.62), channel_id=1, source_target_pairs={{0,56},{8,0},{16,8},{24,16},{32,24},{40,32},{48,40},{56,48},{1,57}... | collective-permute-start | bytes 786440 | tf_op jit(solution)/shard_map/ppermute | solution.py:25
  330.5 11.6 %collective-permute-start.12 = (bf16[128,1024]{1,0:T(8,128)(2,1)S(1)}, bf16[128,1024]{1,0:T(8,128)(2,1)S(1)}, u32[]{:S(2)}, u32[]{:S(2)}) collective-permute-start(bf16[128,1024]{1,0:T(8,128)(2,1)S(1)} %get-tuple-element.61), channel_id=1, source_target_pairs={{0,8},{8,16},{16,24},{24,32},{32,40},{40,48},{48,56},{56,0},{1,9},... | collective-permute-start | bytes 786440 | tf_op jit(solution)/shard_map/ppermute | solution.py:25
  336.8 5.3 %collective-permute-start.16 = (bf16[128,1024]{1,0:T(8,128)(2,1)S(1)}, bf16[128,1024]{1,0:T(8,128)(2,1)S(1)}, u32[]{:S(2)}, u32[]{:S(2)}) collective-permute-start(bf16[128,1024]{1,0:T(8,128)(2,1)S(1)} %add_convert_fusion.1), channel_id=1, source_target_pairs={{0,56},{8,0},{16,8},{24,16},{32,24},{40,32},{48,40},{56,48},{1,57}... | collective-permute-start | bytes 786440 | tf_op jit(solution)/shard_map/ppermute | solution.py:25
Sparse Core Ops, SparseCore 0:
  9.8 41.1 all-gather.3
  52.8 39.8 all-gather.5
  104.5 44.4 reduce-scatter.2
  151.4 47.9 all-gather.7
  255.4 41.3 reduce-scatter.4
